TPU v7x, 256 devices: a whole 4x4x8 slice. The times are simulated.
256 devices in a mesh: lat: 16 (over x, z_lo, core), trc: 16 (over y, z_hi).
Axes of the slice: x: 4, y: 4, z: 8 (z_hi: 4, z_lo: 2; z = z_hi * 2 + z_lo), core: 2. Of those that a mesh axis runs over, the one named last changes fastest.
Arguments:
- tracers: float32 [128, 4, 128, 512], P('trc', None, 'lat'), may hold values from -6 to 6
- transports: float32 [2, 16, 3, 4, 128, 512], P(None, 'trc', None, None, 'lat'), may hold values from -0.1 to 0.1
- thickness: float32 [2, 16, 4, 128, 512], P(None, 'trc', None, 'lat'), may hold values from 1 to 2
- owner: int32 [2], replicated, may hold values from 0 to 15
- land_sea: int32 [128, 512], P('lat'), may hold values 0 or 1
- pairs: int32 [128], P('trc'), may hold values from 0 to 127, as said below
- rates: float32 [128], P('trc'), may hold values from 0.05 to 0.5
Outputs:
- result: float32 [128, 4, 128, 512], P('trc', None, 'lat')
Inputs may be any that keep to these rules, and one draw needn't show every extreme that they name: owner[s] is the index along trc whose record slot holds step s's transports and thicknesses. pairs[i] is a tracer other than i in the same group of 8 consecutive tracers as i, and every tracer is some tracer's partner.
All inputs are finite; a program needn't handle non-finite values. No bound on the sum of `land_sea` on one device may be relied on, other than what follows from the above.
Results may differ from a plain program's by a relative error of at most 0.0003.
Values sent between devices are 32-bit elements; how exact they have to be, the bound alone decides.
A program may use at most 64 MiB of HBM per device.

v0:
```python
import jax
import jax.numpy as jnp
from jax import lax
from jax.sharding import PartitionSpec as P


def with_halo(block, sides, width):
    for axis, dim in sides:
        count = lax.axis_size(axis)
        forward = [(i, i + 1) for i in range(count - 1)]
        backward = [(target, source) for source, target in forward]
        low = lax.ppermute(
            lax.slice_in_dim(block, block.shape[dim] - width, None, axis=dim), axis, forward
        )
        high = lax.ppermute(lax.slice_in_dim(block, 0, width, axis=dim), axis, backward)
        block = jnp.concatenate([low, block, high], axis=dim)
    return block


def broadcast(value, axis, source):
    kept = jnp.where(lax.axis_index(axis) == source, value, 0).astype(value.dtype)
    return lax.psum(kept, axis)


def cut_along(array, start_at, stop_at, along):
    return lax.slice_in_dim(array, start_at, stop_at, axis=array.ndim + along)


def ppm_sweep(tracer_pad, depth_pad, flows, along):
    count = flows.shape[flows.ndim + along] - 1
    left_cell = cut_along(tracer_pad, 1, count + 4, along)
    right_cell = cut_along(tracer_pad, 2, count + 5, along)
    edge_vals = 7.0 / 12.0 * (left_cell + right_cell) - 1.0 / 12.0 * (
        cut_along(tracer_pad, 0, count + 3, along) + cut_along(tracer_pad, 3, count + 6, along)
    )
    edge_vals = jnp.clip(
        edge_vals, jnp.minimum(left_cell, right_cell), jnp.maximum(left_cell, right_cell)
    )
    centre = cut_along(tracer_pad, 2, count + 4, along)
    left_dev = cut_along(edge_vals, 0, count + 2, along) - centre
    right_dev = cut_along(edge_vals, 1, count + 3, along) - centre
    left_lim = jnp.clip(left_dev, -2.0 * jnp.abs(right_dev), 2.0 * jnp.abs(right_dev))
    right_lim = jnp.clip(right_dev, -2.0 * jnp.abs(left_dev), 2.0 * jnp.abs(left_dev))
    left_edge = centre + left_lim
    right_edge = centre + right_lim
    slope_all = right_edge - left_edge
    curv_six = 6.0 * centre - 3.0 * (left_edge + right_edge)
    positive = flows > 0
    depth_up = jnp.where(
        positive,
        cut_along(depth_pad, 0, count + 1, along),
        cut_along(depth_pad, 1, count + 2, along),
    )
    courant = jnp.abs(flows) / jnp.maximum(depth_up, 0.25)
    from_left = cut_along(right_edge, 0, count + 1, along) - 0.5 * courant * (
        cut_along(slope_all, 0, count + 1, along)
        - (1.0 - 2.0 * courant / 3.0) * cut_along(curv_six, 0, count + 1, along)
    )
    from_right = cut_along(left_edge, 1, count + 2, along) + 0.5 * courant * (
        cut_along(slope_all, 1, count + 2, along)
        + (1.0 - 2.0 * courant / 3.0) * cut_along(curv_six, 1, count + 2, along)
    )
    flux_face = flows * jnp.where(positive, from_left, from_right)
    depth_old = cut_along(depth_pad, 1, count + 1, along)
    tracer_old = cut_along(tracer_pad, 3, count + 3, along)
    depth_new = (
        depth_old + cut_along(flows, 0, count, along) - cut_along(flows, 1, count + 1, along)
    )
    content = (
        depth_old * tracer_old
        + cut_along(flux_face, 0, count, along)
        - cut_along(flux_face, 1, count + 1, along)
    )
    return (content / depth_new, depth_new)


def zonal_and_vertical(field, depth, record, sea_mask):
    east_faces = record[0] * (sea_mask * jnp.roll(sea_mask, -1, axis=1))[None]
    flows = jnp.concatenate([east_faces[..., -1:], east_faces], axis=-1)
    tracer_pad = jnp.concatenate([field[..., -3:], field, field[..., :3]], axis=-1)
    depth_pad = jnp.concatenate([depth[..., -1:], depth, depth[..., :1]], axis=-1)
    field, depth = ppm_sweep(tracer_pad, depth_pad, flows, -1)
    tracer_pad = jnp.concatenate([field[:, :1]] * 3 + [field] + [field[:, -1:]] * 3, axis=1)
    depth_pad = jnp.concatenate([depth[:1], depth, depth[-1:]], axis=0)
    down_faces = record[2] * sea_mask[None]
    flows = jnp.concatenate([jnp.zeros_like(down_faces[:1]), down_faces], axis=0)
    field, depth = ppm_sweep(tracer_pad, depth_pad, flows, -3)
    return field


def meridional(field, record, sea_mask):
    north = record[1]
    depth = record[3]
    sea_plane = jnp.broadcast_to(sea_mask[None], depth.shape)
    tracer_pad = with_halo(field, (("lat", 2),), 3)
    small = jnp.stack([north, depth, sea_plane])
    small_pad = with_halo(small, (("lat", 2),), 1)
    north_rows = small_pad[0, :, 1:]
    depth_pad = small_pad[1]
    sea_rows = small_pad[2, 0]
    north_faces = north_rows * (sea_rows[:-1] * sea_rows[1:])[None]
    return ppm_sweep(tracer_pad, depth_pad, north_faces, -2)


def per_device(tracers, transports, thickness, owner, land_sea, pairs, rates):
    sea_mask = land_sea.astype(jnp.float32)
    group_size = tracers.shape[0]
    local_pairs = pairs - lax.axis_index("trc") * group_size
    chooser = (local_pairs[:, None] == jnp.arange(group_size, dtype=jnp.int32)[None, :]).astype(
        jnp.float32
    )
    field = tracers
    for step in range(transports.shape[0]):
        record = jnp.concatenate([transports[step, 0], thickness[step, 0][None]], axis=0)
        record = broadcast(record, "trc", owner[step])
        field, depth = meridional(field, record, sea_mask)
        field = zonal_and_vertical(field, depth, record, sea_mask)
        partner = jnp.einsum("ij,jlrc->ilrc", chooser, field, precision=lax.Precision.HIGHEST)
        field = field + sea_mask[None, None] * rates[:, None, None, None] * (partner - field)
    return field


def solution(mesh):
    placed = (
        P("trc", None, "lat", None),
        P(None, "trc", None, None, "lat", None),
        P(None, "trc", None, "lat", None),
        P(),
        P("lat", None),
        P("trc"),
        P("trc"),
    )
    return jax.shard_map(
        per_device,
        mesh=mesh,
        in_specs=placed,
        out_specs=P("trc", None, "lat", None),
        check_vma=False,
    )
```

profile of v0, /device:TPU:1, one launch (start us, length us, event | category | flops | bytes accessed | tf_op | source)
XLA Modules:
  0.0 236.0 jit_solution(14836258049032879893)
XLA Ops:
  6.5 1.3 copy.8
  7.9 5.1 %collective-permute-start.4 = (f32[8,4,3,512]{3,0,2,1:T(8,128)S(1)}, f32[8,4,3,512]{3,0,2,1:T(8,128)S(1)}, u32[]{:S(2)}, u32[]{:S(2)}) collective-permute-start(f32[8,4,3,512]{3,0,2,1:T(8,128)S(1)} %get-tuple-element.50), channel_id=1, source_target_pairs={{0,16},{16,32},{32,48},{48,64},{64,80},{80,96},{96,112},{112,128},... | collective-permute-start | bytes 589832 | tf_op jit(solution)/shard_map/ppermute | solution.py:12
  13.0 1.9 collective-permute-start.5
  15.0 0.6 copy-done.6
  15.7 0.6 fusion.163
  17.6 0.9 maximum_select_fusion
  18.6 0.6 copy-done.7
  19.4 0.6 copy-done.8
  21.1 158.3 %all-reduce.5.cloned.1.call-done = (f32[4,4,8,512]{3,2,1,0:T(8,128)}, f32[4,4,8,512]{3,2,1,0:T(8,128)}) async-done(((f32[4,4,8,512]{3,2,1,0:T(8,128)}, f32[4,4,8,512]{3,2,1,0:T(8,128)}), (f32[4,4,8,512]{3,2,1,0:T(8,128)}, f32[4,4,8,512]{3,2,1,0:T(8,128)})) %all-reduce.5.cloned.1.call-update) | async-done | bytes 524304 | tf_op jit(solution)/shard_map/psum | solution.py:22
  179.5 0.9 fusion.155
  180.6 12.9 %collective-permute-start.1 = (f32[3,4,1,512]{3,2,1,0:T(1,128)S(1)}, f32[3,4,1,512]{3,2,1,0:T(1,128)S(1)}, u32[]{:S(2)}, u32[]{:S(2)}) collective-permute-start(f32[3,4,1,512]{3,2,1,0:T(1,128)S(1)} %get-tuple-element.66), channel_id=1, source_target_pairs={{16,0},{32,16},{48,32},{64,48},{80,64},{96,80},{112,96},{128,112},... | collective-permute-start | bytes 73736 | tf_op jit(solution)/shard_map/ppermute | solution.py:15
  193.5 2.2 collective-permute-start
  195.7 2.1 collective-permute-start.3
  197.9 3.4 %collective-permute-start.2 = (f32[3,4,1,512]{3,2,1,0:T(1,128)S(1)}, f32[3,4,1,512]{3,2,1,0:T(1,128)S(1)}, u32[]{:S(2)}, u32[]{:S(2)}) collective-permute-start(f32[3,4,1,512]{3,2,1,0:T(1,128)S(1)} %get-tuple-element.67), channel_id=1, source_target_pairs={{0,16},{16,32},{32,48},{48,64},{64,80},{80,96},{96,112},{112,128},... | collective-permute-start | bytes 73736 | tf_op jit(solution)/shard_map/ppermute | solution.py:12
  204.0 0.6 fusion.63
  205.6 0.6 fusion.56
  208.0 0.6 fusion.1
  208.7 4.2 %collective-permute-start.6 = (f32[8,4,3,512]{3,0,2,1:T(8,128)S(1)}, f32[8,4,3,512]{3,0,2,1:T(8,128)S(1)}, u32[]{:S(2)}, u32[]{:S(2)}) collective-permute-start(f32[8,4,3,512]{3,0,2,1:T(8,128)S(1)} %get-tuple-element.44), channel_id=1, source_target_pairs={{0,16},{16,32},{32,48},{48,64},{64,80},{80,96},{96,112},{112,128},... | collective-permute-start | bytes 589832 | tf_op jit(solution)/shard_map/ppermute | solution.py:12
  212.9 2.1 collective-permute-start.7
  215.5 6.4 %collective-permute-done.7 = f32[8,4,3,512]{3,0,2,1:T(8,128)S(1)} collective-permute-done((f32[8,4,3,512]{3,0,2,1:T(8,128)S(1)}, f32[8,4,3,512]{3,0,2,1:T(8,128)S(1)}, u32[]{:S(2)}, u32[]{:S(2)}) %collective-permute-start.7) | collective-permute-done | bytes 196640 | tf_op jit(solution)/shard_map/ppermute | solution.py:15
  223.7 0.6 fusion.67
  225.1 0.6 fusion.40
  227.5 0.6 fusion.3
  228.1 1.1 copy.14
  (101 shorter events, 11.7 us)
Async XLA Ops:
  6.5 172.9 %all-reduce.5.cloned.1.call-start = ((), (), s32[]{:S(2)}) async-start(), calls=%async_computation | async-start | bytes 1048576 | tf_op jit(solution)/shard_map/psum | solution.py:22
  7.9 7.1 %copy-start.4 = (f32[2,1,4,8,512]{4,3,2,1,0:T(8,128)S(1)}, f32[2,1,4,8,512]{4,3,2,1,0:T(8,128)}, u32[]{:S(2)}) copy-start(f32[2,1,4,8,512]{4,3,2,1,0:T(8,128)} %param.9) | copy-start | bytes 393220
  7.9 7.1 %copy-start.1 = (f32[2,1,3,4,8,512]{5,4,3,2,1,0:T(8,128)S(1)}, f32[2,1,3,4,8,512]{5,4,3,2,1,0:T(8,128)}, u32[]{:S(2)}) copy-start(f32[2,1,3,4,8,512]{5,4,3,2,1,0:T(8,128)} %param.8) | copy-start | bytes 1179652
  7.9 12.0 %collective-permute-start.4 = (f32[8,4,3,512]{3,0,2,1:T(8,128)S(1)}, f32[8,4,3,512]{3,0,2,1:T(8,128)S(1)}, u32[]{:S(2)}, u32[]{:S(2)}) collective-permute-start(f32[8,4,3,512]{3,0,2,1:T(8,128)S(1)} %get-tuple-element.50), channel_id=1, source_target_pairs={{0,16},{16,32},{32,48},{48,64},{64,80},{80,96},{96,112},{112,128},... | collective-permute-start | bytes 589832 | tf_op jit(solution)/shard_map/ppermute | solution.py:12
  13.0 7.3 %collective-permute-start.5 = (f32[8,4,3,512]{3,0,2,1:T(8,128)S(1)}, f32[8,4,3,512]{3,0,2,1:T(8,128)S(1)}, u32[]{:S(2)}, u32[]{:S(2)}) collective-permute-start(f32[8,4,3,512]{3,0,2,1:T(8,128)S(1)} %get-tuple-element.49), channel_id=1, source_target_pairs={{16,0},{32,16},{48,32},{64,48},{80,64},{96,80},{112,96},{128,112},... | collective-permute-start | bytes 589832 | tf_op jit(solution)/shard_map/ppermute | solution.py:15
  15.0 0.7 copy-start.6
  17.6 0.9 copy-start.5
  18.4 1.5 copy-start
  18.5 0.7 copy-start.7
  19.3 0.7 copy-start.8
  179.5 1.0 copy-start.2
  180.5 20.8 %copy-start.3 = (f32[4,4,8,512]{3,2,1,0:T(8,128)S(1)}, f32[4,4,8,512]{3,2,1,0:T(8,128)}, u32[]{:S(2)}) copy-start(f32[4,4,8,512]{3,2,1,0:T(8,128)} %get-tuple-element.6) | copy-start | bytes 786436
  180.6 21.1 %collective-permute-start.1 = (f32[3,4,1,512]{3,2,1,0:T(1,128)S(1)}, f32[3,4,1,512]{3,2,1,0:T(1,128)S(1)}, u32[]{:S(2)}, u32[]{:S(2)}) collective-permute-start(f32[3,4,1,512]{3,2,1,0:T(1,128)S(1)} %get-tuple-element.66), channel_id=1, source_target_pairs={{16,0},{32,16},{48,32},{64,48},{80,64},{96,80},{112,96},{128,112},... | collective-permute-start | bytes 73736 | tf_op jit(solution)/shard_map/ppermute | solution.py:15
  193.5 8.4 %collective-permute-start = (f32[3,4,1,512]{3,2,1,0:T(1,128)S(1)}, f32[3,4,1,512]{3,2,1,0:T(1,128)S(1)}, u32[]{:S(2)}, u32[]{:S(2)}) collective-permute-start(f32[3,4,1,512]{3,2,1,0:T(1,128)S(1)} %get-tuple-element.65), channel_id=1, source_target_pairs={{0,16},{16,32},{32,48},{48,64},{64,80},{80,96},{96,112},{112,128},... | collective-permute-start | bytes 73736 | tf_op jit(solution)/shard_map/ppermute | solution.py:12
  195.7 6.0 %collective-permute-start.3 = (f32[3,4,1,512]{3,2,1,0:T(1,128)S(1)}, f32[3,4,1,512]{3,2,1,0:T(1,128)S(1)}, u32[]{:S(2)}, u32[]{:S(2)}) collective-permute-start(f32[3,4,1,512]{3,2,1,0:T(1,128)S(1)} %get-tuple-element.68), channel_id=1, source_target_pairs={{16,0},{32,16},{48,32},{64,48},{80,64},{96,80},{112,96},{128,112},... | collective-permute-start | bytes 73736 | tf_op jit(solution)/shard_map/ppermute | solution.py:15
  197.9 4.4 %collective-permute-start.2 = (f32[3,4,1,512]{3,2,1,0:T(1,128)S(1)}, f32[3,4,1,512]{3,2,1,0:T(1,128)S(1)}, u32[]{:S(2)}, u32[]{:S(2)}) collective-permute-start(f32[3,4,1,512]{3,2,1,0:T(1,128)S(1)} %get-tuple-element.67), channel_id=1, source_target_pairs={{0,16},{16,32},{32,48},{48,64},{64,80},{80,96},{96,112},{112,128},... | collective-permute-start | bytes 73736 | tf_op jit(solution)/shard_map/ppermute | solution.py:12
  208.7 6.8 %collective-permute-start.6 = (f32[8,4,3,512]{3,0,2,1:T(8,128)S(1)}, f32[8,4,3,512]{3,0,2,1:T(8,128)S(1)}, u32[]{:S(2)}, u32[]{:S(2)}) collective-permute-start(f32[8,4,3,512]{3,0,2,1:T(8,128)S(1)} %get-tuple-element.44), channel_id=1, source_target_pairs={{0,16},{16,32},{32,48},{48,64},{64,80},{80,96},{96,112},{112,128},... | collective-permute-start | bytes 589832 | tf_op jit(solution)/shard_map/ppermute | solution.py:12
  212.9 9.0 %collective-permute-start.7 = (f32[8,4,3,512]{3,0,2,1:T(8,128)S(1)}, f32[8,4,3,512]{3,0,2,1:T(8,128)S(1)}, u32[]{:S(2)}, u32[]{:S(2)}) collective-permute-start(f32[8,4,3,512]{3,0,2,1:T(8,128)S(1)} %get-tuple-element.43), channel_id=1, source_target_pairs={{16,0},{32,16},{48,32},{64,48},{80,64},{96,80},{112,96},{128,112},... | collective-permute-start | bytes 589832 | tf_op jit(solution)/shard_map/ppermute | solution.py:15
Sparse Core Ops, SparseCore 0:
  18.6 160.8 all-reduce.4
where the time goes:
time: 237 us; the launch traced here: 236 us
  waiting for transfers between devices  165 us (70%)
  starting transfers between devices  33.9 us (14%)
  between operations  15.4 us (6%)
  other arithmetic  13.2 us (6%)
  local copies, waits for them, and re-layouts  7.03 us (3%)
    psum x1, waiting for transfers between devices, broadcast(): return lax.psum(kept, axis)  158 us
    ppermute x4, starting transfers between devices, with_halo(): lax.ppermute(lax.slice_in_dim(block, 0, width, axis=dim), axis, backward)  19.1 us
    ppermute x4, starting transfers between devices, with_halo(): lax.ppermute(lax.slice_in_dim(block, block.shape[dim] - width, None, axis...  14.9 us
    ppermute x4, waiting for transfers between devices, with_halo(): lax.ppermute(lax.slice_in_dim(block, 0, width, axis=dim), axis, backward)  6.38 us
  transfers between devices with their start and end apart: 9, of which 4 were waited for; matrix products, arithmetic and copies ran while one was open for 2% of the time, Pallas kernels for 0%

commit v1 on v0

v1 whole, which is shorter than its diff:
```python
import functools

import jax
import jax.numpy as jnp
from jax import lax
from jax.experimental import pallas as pl
from jax.experimental.pallas import tpu as pltpu
from jax.sharding import PartitionSpec as P

MESH = pl.DeviceIdType.MESH
TRC, LEV, ROWS, LON, STEPS, RING = 8, 4, 8, 512, 2, 16
BLK = 128
F32 = jnp.float32

GROUPS = (((0, 1), (0, -1)), ((0, 0), (0, 2)), ((1, 1), (1, -1)), ((1, 0), (1, 2)))


def limited(left, right):
    two_l, two_r = 2.0 * jnp.abs(left), 2.0 * jnp.abs(right)
    return (
        jnp.minimum(jnp.maximum(left, -two_r), two_r),
        jnp.minimum(jnp.maximum(right, -two_l), two_l),
    )


def edge_dev(before, here, after):
    dev = 0.5 * here + (1.0 / 12.0) * (before - after)
    return jnp.minimum(jnp.maximum(dev, jnp.minimum(here, 0.0)), jnp.maximum(here, 0.0))


def face_terms(flow, depth_up):
    courant = jnp.abs(flow) / jnp.maximum(depth_up, 0.25)
    rest = 1.0 - courant
    scaled = flow * rest
    return scaled * rest, -courant * scaled


def kernel(
    tracers, transports, thickness, owner, land_sea, pairs, rates, out,
    stage, halo_rec, recv0, recv1, recv2, recv3, recv_halo0, recv_halo1, sel_a, sel_b, rec_a, rec_b, sea_int, sea_halo_int,
    field_a, field_b, mid, mid2, done,
    c_mer, c_zon, c_ver, w_mer, w_zon, w_ver, depth,
    owner_s, pairs_s, rates_s,
    local_sem, send_sem, recv_sem,
):
    recv, recv_halo = (recv0, recv1, recv2, recv3), (recv_halo0, recv_halo1)
    lat, me = lax.axis_index("lat"), lax.axis_index("trc")
    my_y, my_z = me // 4, me % 4
    north, south = lax.rem(lat + 1, RING), lax.rem(lat + RING - 1, RING)

    def lanes(y):
        return pl.ds(pl.multiple_of(y * BLK, BLK), BLK)

    barrier = pltpu.get_barrier_semaphore()

    def greet(k, _):
        peer = lax.rem(me + k, RING)
        pl.semaphore_signal(barrier, inc=1, device_id={"trc": peer}, device_id_type=MESH)
        return 0

    for beside in (north, south):
        pl.semaphore_signal(barrier, inc=1, device_id={"lat": beside}, device_id_type=MESH)
    lax.fori_loop(1, RING, greet, 0)

    stages = []
    for g, fields in enumerate(GROUPS):
        copies = []
        for f, (s, k) in enumerate(fields):
            source = thickness.at[s, 0] if k < 0 else transports.at[s, 0, k]
            for y in range(4):
                copies.append(
                    pltpu.make_async_copy(
                        source.at[:, :, pl.ds(y * BLK, BLK)],
                        stage.at[g, pl.ds(4 * y, 4), f],
                        local_sem.at[8 * g + 4 * f + y],
                    )
                )
        for copy in copies:
            copy.start()
        stages.append(copies)
    smalls = [
        pltpu.make_async_copy(owner, owner_s, local_sem.at[32]),
        pltpu.make_async_copy(pairs, pairs_s, local_sem.at[33]),
        pltpu.make_async_copy(rates, rates_s, local_sem.at[34]),
        pltpu.make_async_copy(land_sea, sea_int, local_sem.at[35]),
    ]
    loads = [
        pltpu.make_async_copy(
            tracers.at[t], field_a.at[:, pl.ds(3, ROWS), t], local_sem.at[36 + t]
        )
        for t in range(TRC)
    ]
    for copy in smalls + loads:
        copy.start()

    pl.semaphore_wait(barrier, RING + 1)

    def to_peers(source, target, sem):
        def one(k, _):
            peer = lax.rem(me + k, RING)
            pltpu.make_async_remote_copy(
                source(peer), target, send_sem.at[sem], recv_sem.at[sem],
                device_id={"trc": peer}, device_id_type=MESH,
            ).start()
            return 0

        lax.fori_loop(1, RING, one, 0)

    def all_bytes(sems, like):
        pltpu.make_async_copy(like, like, sems).wait()

    like15, like30 = recv_halo0.at[pl.ds(0, 15)], recv0.at[pl.ds(0, 15)]
    like45 = stage.at[pl.ds(0, 3), pl.ds(0, 15), 0]

    def beside_copy(source, target, sem, where):
        return pltpu.make_async_remote_copy(
            source, target, send_sem.at[sem], recv_sem.at[sem],
            device_id={"lat": where}, device_id_type=MESH,
        )

    def scatter(g):
        for copy in stages[g]:
            copy.wait()
        to_peers(lambda peer: stage.at[g, peer], recv[g].at[me], g)
        recv[g][me] = stage[g, me]

    scatter(0)
    rows = [
        beside_copy(thickness.at[:, 0, :, pl.ds(7, 1)], halo_rec.at[:, :, pl.ds(0, 1)], 10, north),
        beside_copy(thickness.at[:, 0, :, pl.ds(0, 1)], halo_rec.at[:, :, pl.ds(1, 1)], 11, south),
        beside_copy(transports.at[:, 0, 1, :, pl.ds(0, 1)], halo_rec.at[:, :, pl.ds(2, 1)], 12, south),
        beside_copy(land_sea.at[pl.ds(7, 1)], sea_halo_int.at[pl.ds(0, 1)], 13, north),
        beside_copy(land_sea.at[pl.ds(0, 1)], sea_halo_int.at[pl.ds(1, 1)], 14, south),
    ]
    for copy in rows:
        copy.start()
    scatter(1)
    for copy in rows[:3]:
        copy.wait()
    for s in range(STEPS):
        to_peers(lambda peer: halo_rec.at[s, peer % 4, :, lanes(peer // 4)], recv_halo[s].at[me], 4 + s)
        recv_halo[s][me] = halo_rec[s, my_z, :, lanes(my_y)]
    scatter(2)
    scatter(3)

    def field_halos(field, sem):
        return [
            beside_copy(field.at[:, pl.ds(8, 3)], field.at[:, pl.ds(0, 3)], sem, north),
            beside_copy(field.at[:, pl.ds(3, 3)], field.at[:, pl.ds(11, 3)], sem + 1, south),
        ]

    def clear_ends(field):
        @pl.when(lat == 0)
        def _():
            field[:, 0:3] = jnp.zeros((LEV, 3, TRC, LON), F32)

        @pl.when(lat == RING - 1)
        def _():
            field[:, 11:14] = jnp.zeros((LEV, 3, TRC, LON), F32)

    for copy in loads:
        copy.wait()
    halos = field_halos(field_a, 15)
    for copy in halos:
        copy.start()
    for copy in smalls:
        copy.wait()

    def gather(g):
        s, first = g // 2, g % 2 == 0
        all_bytes(recv_sem.at[g], like30)
        if first:
            all_bytes(recv_sem.at[4 + s], like15)
        from_slot = owner_s[s]
        chosen = recv[g][from_slot]
        if first:
            beside = recv_halo[s][from_slot]
            sel_a[s, 0:2] = chosen
            sel_a[s, 2] = beside
            rec_a[s, 0:2, my_z, :, lanes(my_y)] = chosen
            rec_a[s, 2, my_z, :, lanes(my_y)] = beside
            to_peers(lambda peer: sel_a.at[s], rec_a.at[s, :, my_z, :, lanes(my_y)], 6 + g)
        else:
            sel_b[s] = chosen
            rec_b[s, :, my_z, :, lanes(my_y)] = chosen
            to_peers(lambda peer: sel_b.at[s], rec_b.at[s, :, my_z, :, lanes(my_y)], 6 + g)

    gather(0)
    gather(1)
    gather(2)
    gather(3)

    for copy in rows[3:]:
        copy.wait()
    sub = lax.broadcasted_iota(jnp.int32, (ROWS, LON), 0)
    sea = sea_int[...].astype(F32)
    sea_s = jnp.where(lat > 0, sea_halo_int[0:1].astype(F32), 0.0)
    sea_n = jnp.where(lat < RING - 1, sea_halo_int[1:2].astype(F32), 0.0)
    mask_mer = sea * jnp.where(sub == 0, sea_s, pltpu.roll(sea, 1, axis=0))
    mask_top = sea[7:8] * sea_n
    mask_zon = sea * pltpu.roll(sea, LON - 1, axis=1)
    sub1 = lax.broadcasted_iota(jnp.int32, (TRC, BLK), 0)
    partner = jnp.zeros((TRC, BLK), jnp.int32)
    rate = jnp.zeros((TRC, BLK), F32)
    for i in range(TRC):
        partner = jnp.where(sub1 == i, pairs_s[i] - me * TRC, partner)
        rate = jnp.where(sub1 == i, rates_s[i], rate)

    def mer_terms(s):
        def level(l, _):
            flow0, h, x = rec_a[s, 0, l], rec_a[s, 1, l], rec_a[s, 2, l]
            flow = flow0 * mask_mer
            below = jnp.where(sub == 0, x[0:1], pltpu.roll(h, 1, axis=0))
            near, far = face_terms(flow, jnp.where(flow > 0, below, h))
            c_mer[0, l, 0:8], c_mer[1, l, 0:8], c_mer[2, l, 0:8] = flow, near, far
            top = x[2:3] * mask_top
            near, far = face_terms(top, jnp.where(top > 0, h[7:8], x[1:2]))
            c_mer[0, l, 8:9], c_mer[1, l, 8:9], c_mer[2, l, 8:9] = top, near, far
            h_new = h + flow - jnp.where(sub == 7, top, pltpu.roll(flow, 7, axis=0))
            inv = 1.0 / h_new
            w_mer[0, l], w_mer[1, l] = h * inv, inv
            depth[l] = h_new
            return 0

        lax.fori_loop(0, LEV, level, 0)

    def zon_terms(s):
        def level(l, _):
            h = depth[l]
            east = rec_b[s, 0, l] * mask_zon
            flow = pltpu.roll(east, 1, axis=1)
            near, far = face_terms(flow, jnp.where(flow > 0, pltpu.roll(h, 1, axis=1), h))
            c_zon[0, l], c_zon[1, l], c_zon[2, l] = flow, near, far
            h_new = h + flow - east
            inv = 1.0 / h_new
            w_zon[0, l], w_zon[1, l] = h * inv, inv
            depth[l] = h_new
            return 0

        lax.fori_loop(0, LEV, level, 0)

    def ver_terms(s):
        flow_in = jnp.zeros((ROWS, LON), F32)
        for l in range(LEV):
            h = depth[l]
            flow = rec_b[s, 1, l] * sea
            c_ver[0, l] = flow
            if l < LEV - 1:
                c_ver[1, l], c_ver[2, l] = face_terms(flow, jnp.where(flow > 0, h, depth[l + 1]))
            inv = 1.0 / (h + flow_in - flow)
            w_ver[0, l], w_ver[1, l] = h * inv, inv
            flow_in = flow

    def wide(ref, *at):
        return jnp.broadcast_to(ref[at], (TRC, ref[at].shape[-1]))

    def flux(flow, near, far, q0, r0, l0, q1, l1, r1):
        up = flow > 0
        return (
            flow * jnp.where(up, q0, q1)
            + near * jnp.where(up, r0, l1)
            + far * jnp.where(up, l0, r1)
        )

    def meridional(field):
        def column(i, _):
            l, y = i // 4, lanes(i % 4)
            q = [field[l, j, :, y] for j in range(14)]
            d = [None] + [q[j] - q[j - 1] for j in range(1, 14)]
            e = {f: edge_dev(d[f - 1], d[f], d[f + 1]) for f in range(2, 13)}
            dev = {j: limited(e[j] - d[j], e[j + 1]) for j in range(2, 12)}
            across = []
            for f in range(3, 12):
                r = pl.ds(f - 3, 1)
                terms = [wide(c_mer, k, l, r, y) for k in range(3)]
                (l0, r0), (l1, r1) = dev[f - 1], dev[f]
                across.append(flux(*terms, q[f - 1], r0, l0, q[f], l1, r1))
            for r in range(ROWS):
                kept, inv = (wide(w_mer, k, l, pl.ds(r, 1), y) for k in range(2))
                mid[l, r, :, y] = kept * q[r + 3] + inv * (across[r] - across[r + 1])
            return 0

        lax.fori_loop(0, LEV * 4, column, 0)

    def zonal_row(r):
        def level(l, _):
            q = mid[l, r]
            before = pltpu.roll(q, 1, axis=1)
            d = q - before
            e = edge_dev(pltpu.roll(d, 1, axis=1), d, pltpu.roll(d, LON - 1, axis=1))
            left, right = limited(e - d, pltpu.roll(e, LON - 1, axis=1))
            at = pl.ds(r, 1)
            terms = [wide(c_zon, k, l, at) for k in range(3)]
            across = flux(*terms, before, pltpu.roll(right, 1, axis=1), pltpu.roll(left, 1, axis=1), q, left, right)
            kept, inv = (wide(w_zon, k, l, at) for k in range(2))
            mid2[l] = kept * q + inv * (across - pltpu.roll(across, LON - 1, axis=1))
            return 0

        lax.fori_loop(0, LEV, level, 0)

    def vertical_row(r, target, offset):
        def block(b, _):
            y, at = lanes(b), pl.ds(r, 1)
            q = [mid2[l, :, y] for l in range(LEV)]
            none = jnp.zeros((TRC, BLK), F32)
            d = [none] + [q[l] - q[l - 1] for l in range(1, LEV)] + [none]
            e = [none] + [edge_dev(d[f - 1], d[f], d[f + 1]) for f in range(1, LEV)] + [none]
            dev = [(none, none)] + [limited(e[l] - d[l], e[l + 1]) for l in range(1, LEV - 1)] + [(none, none)]
            across = [None]
            for f in range(1, LEV):
                terms = [wide(c_ver, k, f - 1, at, y) for k in range(3)]
                (l0, r0), (l1, r1) = dev[f - 1], dev[f]
                across.append(flux(*terms, q[f - 1], r0, l0, q[f], l1, r1))
            across.append(wide(c_ver, 0, LEV - 1, at, y) * q[LEV - 1])
            share = rate * jnp.broadcast_to(sea_f[at, y], (TRC, BLK))
            for l in range(LEV):
                kept, inv = (wide(w_ver, k, l, at, y) for k in range(2))
                gain = -across[l + 1] if l == 0 else across[l] - across[l + 1]
                new = kept * q[l] + inv * gain
                other = jnp.take_along_axis(new, partner, axis=0)
                target[l, offset + r, :, y] = new + share * (other - new)
            return 0

        lax.fori_loop(0, 4, block, 0)

    sea_f = depth.at[LEV]
    sea_f[...] = sea

    def run_rows(first, last, target, offset):
        for r in range(first, last):
            zonal_row(r)
            vertical_row(r, target, offset)

    all_bytes(recv_sem.at[6], like45)
    mer_terms(0)
    for copy in halos:
        copy.wait()
    clear_ends(field_a)
    meridional(field_a)
    all_bytes(recv_sem.at[7], like30)
    zon_terms(0)
    ver_terms(0)
    halos = field_halos(field_b, 17)
    run_rows(0, 3, field_b, 3)
    halos[1].start()
    run_rows(5, 8, field_b, 3)
    halos[0].start()
    run_rows(3, 5, field_b, 3)

    all_bytes(recv_sem.at[8], like45)
    mer_terms(1)
    for copy in halos:
        copy.wait()
    clear_ends(field_b)
    meridional(field_b)
    all_bytes(recv_sem.at[9], like30)
    zon_terms(1)
    ver_terms(1)
    run_rows(0, ROWS, done, 0)
    stores = [
        pltpu.make_async_copy(done.at[:, :, t], out.at[t], local_sem.at[36 + t])
        for t in range(TRC)
    ]
    for copy in stores:
        copy.start()
    for g, like in ((0, like30), (1, like30), (2, like30), (3, like30), (4, like15), (5, like15),
                    (6, like45), (7, like30), (8, like45), (9, like30)):
        all_bytes(send_sem.at[g], like)
    for copy in stores:
        copy.wait()


def per_device(*args):
    any_space = pl.BlockSpec(memory_space=pl.ANY)
    vmem = pltpu.VMEM
    return pl.pallas_call(
        kernel,
        out_shape=jax.ShapeDtypeStruct((TRC, LEV, ROWS, LON), F32),
        in_specs=[any_space] * 7,
        out_specs=any_space,
        scratch_shapes=[
            vmem((4, RING, 2, ROWS, BLK), F32),
            vmem((STEPS, LEV, ROWS, LON), F32),
            *[vmem((RING, 2, ROWS, BLK), F32)] * 4,
            *[vmem((RING, ROWS, BLK), F32)] * STEPS,
            vmem((STEPS, 3, ROWS, BLK), F32),
            vmem((STEPS, 2, ROWS, BLK), F32),
            vmem((STEPS, 3, LEV, ROWS, LON), F32),
            vmem((STEPS, 2, LEV, ROWS, LON), F32),
            vmem((ROWS, LON), jnp.int32),
            vmem((ROWS, LON), jnp.int32),
            vmem((LEV, 14, TRC, LON), F32),
            vmem((LEV, 14, TRC, LON), F32),
            vmem((LEV, ROWS, TRC, LON), F32),
            vmem((LEV, TRC, LON), F32),
            vmem((LEV, ROWS, TRC, LON), F32),
            vmem((3, LEV, 2 * ROWS, LON), F32),
            vmem((3, LEV, ROWS, LON), F32),
            vmem((3, LEV, ROWS, LON), F32),
            vmem((2, LEV, ROWS, LON), F32),
            vmem((2, LEV, ROWS, LON), F32),
            vmem((2, LEV, ROWS, LON), F32),
            vmem((LEV + 1, ROWS, LON), F32),
            pltpu.SMEM((STEPS,), jnp.int32),
            pltpu.SMEM((TRC,), jnp.int32),
            pltpu.SMEM((TRC,), F32),
            pltpu.SemaphoreType.DMA((44,)),
            pltpu.SemaphoreType.DMA((19,)),
            pltpu.SemaphoreType.DMA((19,)),
        ],
        compiler_params=pltpu.CompilerParams(
            collective_id=0, has_side_effects=True, vmem_limit_bytes=32 * 1024 * 1024
        ),
    )(*args)


def solution(mesh):
    placed = (
        P("trc", None, "lat", None),
        P(None, "trc", None, None, "lat", None),
        P(None, "trc", None, "lat", None),
        P(),
        P("lat", None),
        P("trc"),
        P("trc"),
    )
    return jax.shard_map(
        per_device,
        mesh=mesh,
        in_specs=placed,
        out_specs=P("trc", None, "lat", None),
        check_vma=False,
    )
```

time: 237 us -> 77.5 us (0.33)
  waiting for transfers between devices: 165 us -> 0 us
  Pallas kernels: 0 us -> 69.7 us
  starting transfers between devices: 33.9 us -> 0 us
  between operations: 15.4 us -> 0.02 us
  other arithmetic: 13.2 us -> 0 us
    psum x1 -> x0, waiting for transfers between devices: 158 us -> none  [broadcast(): return lax.psum(kept, axis)]
    pallas_call x0 -> x1, Pallas kernels: none -> 69.7 us  [per_device(): pl.pallas_call(kernel, out_shape=jax.ShapeDtypeStruct((TRC, LEV, ROWS, LO...]
    ppermute x8 -> x0, starting transfers between devices: 33.9 us -> none  [the longest x4 19.1 us: with_halo(): lax.ppermute(lax.slice_in_dim(block, 0, width, axis=dim), axis, backward)]
    ppermute x8 -> x0, waiting for transfers between devices: 6.96 us -> none  [the longest x4 6.38 us: with_halo(): lax.ppermute(lax.slice_in_dim(block, 0, width, axis=dim), axis, backward)]
    sub x17 -> x0, other arithmetic: 4.24 us -> none  [the longest x6 2.38 us: ppm_sweep(): slope_all = right_edge - left_edge]
    mul x18 -> x0, other arithmetic: 3.67 us -> none  [the longest x8 3.05 us: ppm_sweep(): flux_face = flows * jnp.where(positive, from_left, from_right)]
    unnamed x21 -> x15, local copies, waits for them, and re-layouts: 3.63 us -> 6.42 us
  transfers between devices with their start and end apart: 9 -> 0, of which waited for: 4 -> 0; matrix products, arithmetic and copies ran while one was open for 2% -> 0% of each run, Pallas kernels for 0% -> 0%
where the time goes in v1:
time: 77.5 us; the launch traced here: 76.2 us
  Pallas kernels  69.7 us (90%)
  local copies, waits for them, and re-layouts  6.42 us (8%)
    pallas_call x1, Pallas kernels, per_device(): pl.pallas_call(kernel, out_shape=jax.ShapeDtypeStruct((TRC, LEV, ROWS, LO...  69.7 us
    unnamed x15, local copies, waits for them, and re-layouts  6.42 us

profile of v1, /device:TPU:1, one launch (start us, length us, event | category | flops | bytes accessed | tf_op | source)
XLA Modules:
  0.0 76.2 jit_solution(11820267244842392565)
XLA Ops:
  0.0 0.0 copy-start
  0.0 1.0 %copy-done = f32[8,4,8,512]{3,2,1,0:T(8,128)S(1)} copy-done((f32[8,4,8,512]{3,2,1,0:T(8,128)S(1)}, f32[8,4,8,512]{3,2,1,0:T(8,128)}, u32[]{:S(2)}) %copy-start) | copy-done | bytes 524312
  1.0 0.0 copy-start.1
  1.0 1.0 %copy-done.1 = f32[2,1,3,4,8,512]{5,4,3,2,1,0:T(8,128)S(1)} copy-done((f32[2,1,3,4,8,512]{5,4,3,2,1,0:T(8,128)S(1)}, f32[2,1,3,4,8,512]{5,4,3,2,1,0:T(8,128)}, u32[]{:S(2)}) %copy-start.1) | copy-done | bytes 393240
  2.0 0.0 copy-start.2
  2.0 0.9 %copy-done.2 = f32[2,1,4,8,512]{4,3,2,1,0:T(8,128)S(1)} copy-done((f32[2,1,4,8,512]{4,3,2,1,0:T(8,128)S(1)}, f32[2,1,4,8,512]{4,3,2,1,0:T(8,128)}, u32[]{:S(2)}) %copy-start.2) | copy-done | bytes 131096
  2.9 0.0 copy-start.3
  2.9 0.7 copy-done.3
  3.7 0.0 copy-start.4
  3.7 0.7 copy-done.4
  4.3 0.0 copy-start.5
  4.3 0.7 copy-done.5
  5.0 0.0 copy-start.6
  5.0 0.7 copy-done.6
  5.6 69.7 %shard_map.73 = f32[8,4,8,512]{3,2,1,0:T(8,128)S(1)} custom-call(f32[8,4,8,512]{3,2,1,0:T(8,128)S(1)} %copy-done, f32[2,1,3,4,8,512]{5,4,3,2,1,0:T(8,128)S(1)} %copy-done.1, f32[2,1,4,8,512]{4,3,2,1,0:T(8,128)S(1)} %copy-done.2, s32[2]{0:T(128)S(1)} %copy-done.4, s32[8,512]{1,0:T(8,128)S(1)} %copy-done.3, s32[8]{0:T(128)S(1)} %copy-done.5, f32[8]{0:T(128)S(1)} %copy-done.6), custom_call_target="tpu_custom_call" | custom-call | tf_op jit(solution)/shard_map/pallas_call | solution.py:376
  75.4 0.8 %copy.9 = f32[8,4,8,512]{3,2,1,0:T(8,128)} copy(f32[8,4,8,512]{3,2,1,0:T(8,128)S(1)} %shard_map.73) | data formatting | bytes 1048576
Async XLA Ops:
  0.0 1.0 %copy-start = (f32[8,4,8,512]{3,2,1,0:T(8,128)S(1)}, f32[8,4,8,512]{3,2,1,0:T(8,128)}, u32[]{:S(2)}) copy-start(f32[8,4,8,512]{3,2,1,0:T(8,128)} %tracers.1) | copy-start | bytes 1572868
  1.0 1.0 %copy-start.1 = (f32[2,1,3,4,8,512]{5,4,3,2,1,0:T(8,128)S(1)}, f32[2,1,3,4,8,512]{5,4,3,2,1,0:T(8,128)}, u32[]{:S(2)}) copy-start(f32[2,1,3,4,8,512]{5,4,3,2,1,0:T(8,128)} %transports.1) | copy-start | bytes 1179652
  2.0 0.9 %copy-start.2 = (f32[2,1,4,8,512]{4,3,2,1,0:T(8,128)S(1)}, f32[2,1,4,8,512]{4,3,2,1,0:T(8,128)}, u32[]{:S(2)}) copy-start(f32[2,1,4,8,512]{4,3,2,1,0:T(8,128)} %thickness.1) | copy-start | bytes 393220
  2.9 0.7 copy-start.3
  3.7 0.7 copy-start.4
  4.3 0.7 copy-start.5
  5.0 0.7 copy-start.6

commit v2 on v1

--- a/solution.py
+++ b/solution.py
@@ -14,6 +14,8 @@
 
 GROUPS = (((0, 1), (0, -1)), ((0, 0), (0, 2)), ((1, 1), (1, -1)), ((1, 0), (1, 2)))
 
+TILES = (3, 2, 3, 2)
+
 
 def limited(left, right):
     two_l, two_r = 2.0 * jnp.abs(left), 2.0 * jnp.abs(right)
@@ -37,13 +39,15 @@
 
 def kernel(
     tracers, transports, thickness, owner, land_sea, pairs, rates, out,
-    stage, halo_rec, recv0, recv1, recv2, recv3, recv_halo0, recv_halo1, sel_a, sel_b, rec_a, rec_b, sea_int, sea_halo_int,
+    stage, halo_rec, recv0, recv_halo0, along_y1, along_y2, along_y3, along_z1, along_z2, along_z3,
+    quarter1, quarter2, quarter3, part1, part2, part3, sel, rec_a, rec_b, sea_int, sea_halo_int,
     field_a, field_b, mid, mid2, done,
     c_mer, c_zon, c_ver, w_mer, w_zon, w_ver, depth,
     owner_s, pairs_s, rates_s,
     local_sem, send_sem, recv_sem,
 ):
-    recv, recv_halo = (recv0, recv1, recv2, recv3), (recv_halo0, recv_halo1)
+    along_y, along_z = (None, along_y1, along_y2, along_y3), (None, along_z1, along_z2, along_z3)
+    quarter, part = (None, quarter1, quarter2, quarter3), (None, part1, part2, part3)
     lat, me = lax.axis_index("lat"), lax.axis_index("trc")
     my_y, my_z = me // 4, me % 4
     north, south = lax.rem(lat + 1, RING), lax.rem(lat + RING - 1, RING)
@@ -95,58 +99,102 @@
 
     pl.semaphore_wait(barrier, RING + 1)
 
+    def one_copy(source, target, sem, **where):
+        return pltpu.make_async_remote_copy(
+            source, target, send_sem.at[sem], recv_sem.at[sem], device_id=where, device_id_type=MESH
+        )
+
     def to_peers(source, target, sem):
         def one(k, _):
             peer = lax.rem(me + k, RING)
-            pltpu.make_async_remote_copy(
-                source(peer), target, send_sem.at[sem], recv_sem.at[sem],
-                device_id={"trc": peer}, device_id_type=MESH,
-            ).start()
+            one_copy(source(peer), target, sem, trc=peer).start()
             return 0
 
         lax.fori_loop(1, RING, one, 0)
+
+    def along(axis, source, target, sem):
+        for k in (2, 1, 3):
+            if axis == "y":
+                at = lax.rem(my_y + k, 4)
+                one_copy(source(at), target, sem, trc=at * 4 + my_z).start()
+            else:
+                at = lax.rem(my_z + k, 4)
+                one_copy(source(at), target, sem, trc=my_y * 4 + at).start()
 
     def all_bytes(sems, like):
         pltpu.make_async_copy(like, like, sems).wait()
 
-    like15, like30 = recv_halo0.at[pl.ds(0, 15)], recv0.at[pl.ds(0, 15)]
-    like45 = stage.at[pl.ds(0, 3), pl.ds(0, 15), 0]
-
-    def beside_copy(source, target, sem, where):
-        return pltpu.make_async_remote_copy(
-            source, target, send_sem.at[sem], recv_sem.at[sem],
-            device_id={"lat": where}, device_id_type=MESH,
-        )
-
-    def scatter(g):
+    three = pl.ds(0, 3)
+    likes = {0: recv0.at[pl.ds(0, 15)], 1: recv_halo0.at[pl.ds(0, 15)], 2: stage.at[three, pl.ds(0, 15), 0]}
+    for g in (1, 2, 3):
+        first = 8 + 4 * g
+        likes[first] = likes[first + 3] = along_y[g].at[three]
+        likes[first + 1] = likes[first + 2] = along_z[g].at[three]
+
+    def arrived(sem):
+        all_bytes(recv_sem.at[sem], likes[sem])
+
+    def staged(g):
         for copy in stages[g]:
             copy.wait()
-        to_peers(lambda peer: stage.at[g, peer], recv[g].at[me], g)
-        recv[g][me] = stage[g, me]
-
-    scatter(0)
+
+    def scatter_y(g):
+        staged(g)
+        own = pl.ds(4 * my_y, 4)
+        if TILES[g] == 3:
+            along("y", lambda y: stage.at[g, pl.ds(4 * y, 4)], along_y[g].at[my_y, :, pl.ds(0, 2)], 8 + 4 * g)
+            along("y", lambda y: halo_rec.at[1, :, :, lanes(y)], along_y[g].at[my_y, :, 2], 8 + 4 * g)
+            along_y[g][my_y, :, 0:2] = stage[g, own]
+            along_y[g][my_y, :, 2] = halo_rec[1, :, :, lanes(my_y)]
+        else:
+            along("y", lambda y: stage.at[g, pl.ds(4 * y, 4)], along_y[g].at[my_y], 8 + 4 * g)
+            along_y[g][my_y] = stage[g, own]
+
+    def scatter_z(g):
+        arrived(8 + 4 * g)
+        quarter[g][...] = along_y[g][owner_s[g // 2] // 4]
+        along("z", lambda z: quarter[g].at[z], along_z[g].at[my_z], 9 + 4 * g)
+        along_z[g][my_z] = quarter[g][my_z]
+
+    def gather_z(g):
+        arrived(9 + 4 * g)
+        part[g][my_z] = along_z[g][lax.rem(owner_s[g // 2], 4)]
+        along("z", lambda z: part[g].at[my_z], part[g].at[my_z], 10 + 4 * g)
+
+    def gather_y(g):
+        arrived(10 + 4 * g)
+        rec = (rec_a if TILES[g] == 3 else rec_b).at[g // 2]
+        along("y", lambda y: part[g], rec.at[:, :, :, lanes(my_y)], 11 + 4 * g)
+        rec[:, :, :, lanes(my_y)] = part[g][...]
+
+    staged(0)
+    to_peers(lambda peer: stage.at[0, peer], recv0.at[me], 0)
+    recv0[me] = stage[0, me]
+    one, top = pl.ds(0, 1), pl.ds(7, 1)
     rows = [
-        beside_copy(thickness.at[:, 0, :, pl.ds(7, 1)], halo_rec.at[:, :, pl.ds(0, 1)], 10, north),
-        beside_copy(thickness.at[:, 0, :, pl.ds(0, 1)], halo_rec.at[:, :, pl.ds(1, 1)], 11, south),
-        beside_copy(transports.at[:, 0, 1, :, pl.ds(0, 1)], halo_rec.at[:, :, pl.ds(2, 1)], 12, south),
-        beside_copy(land_sea.at[pl.ds(7, 1)], sea_halo_int.at[pl.ds(0, 1)], 13, north),
-        beside_copy(land_sea.at[pl.ds(0, 1)], sea_halo_int.at[pl.ds(1, 1)], 14, south),
+        one_copy(thickness.at[:, 0, :, top], halo_rec.at[:, :, pl.ds(0, 1)], 3, lat=north),
+        one_copy(thickness.at[:, 0, :, one], halo_rec.at[:, :, pl.ds(1, 1)], 4, lat=south),
+        one_copy(transports.at[:, 0, 1, :, one], halo_rec.at[:, :, pl.ds(2, 1)], 5, lat=south),
+        one_copy(land_sea.at[top], sea_halo_int.at[pl.ds(0, 1)], 6, lat=north),
+        one_copy(land_sea.at[one], sea_halo_int.at[pl.ds(1, 1)], 7, lat=south),
     ]
     for copy in rows:
         copy.start()
-    scatter(1)
+    scatter_y(1)
+    for copy in smalls:
+        copy.wait()
     for copy in rows[:3]:
         copy.wait()
-    for s in range(STEPS):
-        to_peers(lambda peer: halo_rec.at[s, peer % 4, :, lanes(peer // 4)], recv_halo[s].at[me], 4 + s)
-        recv_halo[s][me] = halo_rec[s, my_z, :, lanes(my_y)]
-    scatter(2)
-    scatter(3)
+    to_peers(lambda peer: halo_rec.at[0, peer % 4, :, lanes(peer // 4)], recv_halo0.at[me], 1)
+    recv_halo0[me] = halo_rec[0, my_z, :, lanes(my_y)]
+    scatter_y(2)
+    scatter_y(3)
+    scatter_z(1)
 
     def field_halos(field, sem):
         return [
-            beside_copy(field.at[:, pl.ds(8, 3)], field.at[:, pl.ds(0, 3)], sem, north),
-            beside_copy(field.at[:, pl.ds(3, 3)], field.at[:, pl.ds(11, 3)], sem + 1, south),
+            one_copy(field.at[:, pl.ds(8, 3)], field.at[:, pl.ds(0, 3)], sem, lat=north),
+            one_copy(field.at[:, pl.ds(3, 3)], field.at[:, pl.ds(11, 3)], sem + 1, lat=south),
         ]
 
     def clear_ends(field):
@@ -160,38 +208,25 @@
 
     for copy in loads:
         copy.wait()
-    halos = field_halos(field_a, 15)
+    halos = field_halos(field_a, 8)
     for copy in halos:
         copy.start()
-    for copy in smalls:
-        copy.wait()
-
-    def gather(g):
-        s, first = g // 2, g % 2 == 0
-        all_bytes(recv_sem.at[g], like30)
-        if first:
-            all_bytes(recv_sem.at[4 + s], like15)
-        from_slot = owner_s[s]
-        chosen = recv[g][from_slot]
-        if first:
-            beside = recv_halo[s][from_slot]
-            sel_a[s, 0:2] = chosen
-            sel_a[s, 2] = beside
-            rec_a[s, 0:2, my_z, :, lanes(my_y)] = chosen
-            rec_a[s, 2, my_z, :, lanes(my_y)] = beside
-            to_peers(lambda peer: sel_a.at[s], rec_a.at[s, :, my_z, :, lanes(my_y)], 6 + g)
-        else:
-            sel_b[s] = chosen
-            rec_b[s, :, my_z, :, lanes(my_y)] = chosen
-            to_peers(lambda peer: sel_b.at[s], rec_b.at[s, :, my_z, :, lanes(my_y)], 6 + g)
-
-    gather(0)
-    gather(1)
-    gather(2)
-    gather(3)
+
+    arrived(0)
+    arrived(1)
+    sel[0:2] = recv0[owner_s[0]]
+    sel[2] = recv_halo0[owner_s[0]]
+    to_peers(lambda peer: sel, rec_a.at[0, my_z, :, :, lanes(my_y)], 2)
+    rec_a[0, my_z, :, :, lanes(my_y)] = sel[...]
+    scatter_z(2)
+    scatter_z(3)
+    gather_z(1)
+    gather_z(2)
+    gather_z(3)
+    gather_y(1)
 
     for copy in rows[3:]:
-        copy.wait()
+        copy.wait_recv()
     sub = lax.broadcasted_iota(jnp.int32, (ROWS, LON), 0)
     sea = sea_int[...].astype(F32)
     sea_s = jnp.where(lat > 0, sea_halo_int[0:1].astype(F32), 0.0)
@@ -208,7 +243,7 @@
 
     def mer_terms(s):
         def level(l, _):
-            flow0, h, x = rec_a[s, 0, l], rec_a[s, 1, l], rec_a[s, 2, l]
+            flow0, h, x = rec_a[s, l, 0], rec_a[s, l, 1], rec_a[s, l, 2]
             flow = flow0 * mask_mer
             below = jnp.where(sub == 0, x[0:1], pltpu.roll(h, 1, axis=0))
             near, far = face_terms(flow, jnp.where(flow > 0, below, h))
@@ -227,12 +262,16 @@
     def zon_terms(s):
         def level(l, _):
             h = depth[l]
-            east = rec_b[s, 0, l] * mask_zon
-            flow = pltpu.roll(east, 1, axis=1)
-            near, far = face_terms(flow, jnp.where(flow > 0, pltpu.roll(h, 1, axis=1), h))
-            c_zon[0, l], c_zon[1, l], c_zon[2, l] = flow, near, far
-            h_new = h + flow - east
+            east = rec_b[s, l, 0] * mask_zon
+            west = pltpu.roll(east, 1, axis=1)
+            h_new = h + west - east
             inv = 1.0 / h_new
+            flow = jnp.maximum(east, 0.0)
+            c_zon[0, l] = flow
+            c_zon[1, l], c_zon[2, l] = face_terms(flow, h)
+            flow = jnp.minimum(west, 0.0)
+            c_zon[3, l] = flow
+            c_zon[4, l], c_zon[5, l] = face_terms(flow, h)
             w_zon[0, l], w_zon[1, l] = h * inv, inv
             depth[l] = h_new
             return 0
@@ -243,7 +282,7 @@
         flow_in = jnp.zeros((ROWS, LON), F32)
         for l in range(LEV):
             h = depth[l]
-            flow = rec_b[s, 1, l] * sea
+            flow = rec_b[s, l, 1] * sea
             c_ver[0, l] = flow
             if l < LEV - 1:
                 c_ver[1, l], c_ver[2, l] = face_terms(flow, jnp.where(flow > 0, h, depth[l + 1]))
@@ -282,21 +321,32 @@
 
         lax.fori_loop(0, LEV * 4, column, 0)
 
+    lane = lax.broadcasted_iota(jnp.int32, (TRC, BLK), 1)
+
+    def shifted(tiles, by):
+        turned = [pltpu.roll(tile, -by % BLK, axis=1) for tile in tiles]
+        inside = lane < BLK - by if by > 0 else lane >= -by
+        step = 1 if by > 0 else -1
+        return [jnp.where(inside, turned[b], turned[(b + step) % 4]) for b in range(4)]
+
     def zonal_row(r):
-        def level(l, _):
-            q = mid[l, r]
-            before = pltpu.roll(q, 1, axis=1)
-            d = q - before
-            e = edge_dev(pltpu.roll(d, 1, axis=1), d, pltpu.roll(d, LON - 1, axis=1))
-            left, right = limited(e - d, pltpu.roll(e, LON - 1, axis=1))
-            at = pl.ds(r, 1)
-            terms = [wide(c_zon, k, l, at) for k in range(3)]
-            across = flux(*terms, before, pltpu.roll(right, 1, axis=1), pltpu.roll(left, 1, axis=1), q, left, right)
-            kept, inv = (wide(w_zon, k, l, at) for k in range(2))
-            mid2[l] = kept * q + inv * (across - pltpu.roll(across, LON - 1, axis=1))
-            return 0
-
-        lax.fori_loop(0, LEV, level, 0)
+        at = pl.ds(r, 1)
+        for l in range(LEV):
+            q = [mid[l, r, :, b * BLK : (b + 1) * BLK] for b in range(4)]
+            west2, west, east, east2 = (shifted(q, by) for by in (-2, -1, 1, 2))
+            out_east, out_west = [], []
+            for b in range(4):
+                d_w, d, d_e, d_ee = west[b] - west2[b], q[b] - west[b], east[b] - q[b], east2[b] - east[b]
+                left, right = limited(edge_dev(d_w, d, d_e) - d, edge_dev(d, d_e, d_ee))
+                v0, n0, f0, v1, n1, f1 = (wide(c_zon, k, l, at, pl.ds(b * BLK, BLK)) for k in range(6))
+                out_east.append(v0 * q[b] + n0 * right + f0 * left)
+                out_west.append(v1 * q[b] + n1 * left + f1 * right)
+            from_west, from_east = shifted(out_east, -1), shifted(out_west, 1)
+            for b in range(4):
+                y = pl.ds(b * BLK, BLK)
+                kept, inv = (wide(w_zon, k, l, at, y) for k in range(2))
+                gain = (from_west[b] - out_east[b]) + (out_west[b] - from_east[b])
+                mid2[l, :, y] = kept * q[b] + inv * gain
 
     def vertical_row(r, target, offset):
         def block(b, _):
@@ -331,29 +381,31 @@
             zonal_row(r)
             vertical_row(r, target, offset)
 
-    all_bytes(recv_sem.at[6], like45)
+    arrived(2)
     mer_terms(0)
     for copy in halos:
         copy.wait()
     clear_ends(field_a)
     meridional(field_a)
-    all_bytes(recv_sem.at[7], like30)
+    gather_y(2)
+    gather_y(3)
+    arrived(15)
     zon_terms(0)
     ver_terms(0)
-    halos = field_halos(field_b, 17)
+    halos = field_halos(field_b, 10)
     run_rows(0, 3, field_b, 3)
     halos[1].start()
     run_rows(5, 8, field_b, 3)
     halos[0].start()
     run_rows(3, 5, field_b, 3)
 
-    all_bytes(recv_sem.at[8], like45)
+    arrived(19)
     mer_terms(1)
     for copy in halos:
         copy.wait()
     clear_ends(field_b)
     meridional(field_b)
-    all_bytes(recv_sem.at[9], like30)
+    arrived(23)
     zon_terms(1)
     ver_terms(1)
     run_rows(0, ROWS, done, 0)
@@ -363,9 +415,10 @@
     ]
     for copy in stores:
         copy.start()
-    for g, like in ((0, like30), (1, like30), (2, like30), (3, like30), (4, like15), (5, like15),
-                    (6, like45), (7, like30), (8, like45), (9, like30)):
-        all_bytes(send_sem.at[g], like)
+    for sem, like in likes.items():
+        all_bytes(send_sem.at[sem], like)
+    for copy in rows[3:]:
+        copy.wait_send()
     for copy in stores:
         copy.wait()
 
@@ -381,12 +434,15 @@
         scratch_shapes=[
             vmem((4, RING, 2, ROWS, BLK), F32),
             vmem((STEPS, LEV, ROWS, LON), F32),
-            *[vmem((RING, 2, ROWS, BLK), F32)] * 4,
-            *[vmem((RING, ROWS, BLK), F32)] * STEPS,
-            vmem((STEPS, 3, ROWS, BLK), F32),
-            vmem((STEPS, 2, ROWS, BLK), F32),
-            vmem((STEPS, 3, LEV, ROWS, LON), F32),
-            vmem((STEPS, 2, LEV, ROWS, LON), F32),
+            vmem((RING, 2, ROWS, BLK), F32),
+            vmem((RING, ROWS, BLK), F32),
+            *[vmem((4, 4, n, ROWS, BLK), F32) for n in TILES[1:]],
+            *[vmem((4, n, ROWS, BLK), F32) for n in TILES[1:]],
+            *[vmem((4, n, ROWS, BLK), F32) for n in TILES[1:]],
+            *[vmem((4, n, ROWS, BLK), F32) for n in TILES[1:]],
+            vmem((3, ROWS, BLK), F32),
+            vmem((STEPS, LEV, 3, ROWS, LON), F32),
+            vmem((STEPS, LEV, 2, ROWS, LON), F32),
             vmem((ROWS, LON), jnp.int32),
             vmem((ROWS, LON), jnp.int32),
             vmem((LEV, 14, TRC, LON), F32),
@@ -395,7 +451,7 @@
             vmem((LEV, TRC, LON), F32),
             vmem((LEV, ROWS, TRC, LON), F32),
             vmem((3, LEV, 2 * ROWS, LON), F32),
-            vmem((3, LEV, ROWS, LON), F32),
+            vmem((6, LEV, ROWS, LON), F32),
             vmem((3, LEV, ROWS, LON), F32),
             vmem((2, LEV, ROWS, LON), F32),
             vmem((2, LEV, ROWS, LON), F32),
@@ -405,11 +461,11 @@
             pltpu.SMEM((TRC,), jnp.int32),
             pltpu.SMEM((TRC,), F32),
             pltpu.SemaphoreType.DMA((44,)),
-            pltpu.SemaphoreType.DMA((19,)),
-            pltpu.SemaphoreType.DMA((19,)),
+            pltpu.SemaphoreType.DMA((24,)),
+            pltpu.SemaphoreType.DMA((24,)),
         ],
         compiler_params=pltpu.CompilerParams(
-            collective_id=0, has_side_effects=True, vmem_limit_bytes=32 * 1024 * 1024
+            collective_id=0, has_side_effects=True, vmem_limit_bytes=60 * 1024 * 1024
         ),
     )(*args)
 

time: 77.5 us -> 50.9 us (0.66); the launches traced: 76.2 us -> 50.8 us
  Pallas kernels: 69.7 us -> 48.9 us
  local copies, waits for them, and re-layouts: 6.42 us -> 1.87 us
    pallas_call x1, Pallas kernels: 69.7 us -> 48.9 us  [per_device(): pl.pallas_call(kernel, out_shape=jax.ShapeDtypeStruct((TRC, LEV, ROWS, LO...]
    unnamed x15 -> x1, local copies, waits for them, and re-layouts: 6.42 us -> 1.87 us
where the time goes in v2:
time: 50.9 us; the launch traced here: 50.8 us
  Pallas kernels  48.9 us (96%)
  local copies, waits for them, and re-layouts  1.87 us (4%)
    pallas_call x1, Pallas kernels, per_device(): pl.pallas_call(kernel, out_shape=jax.ShapeDtypeStruct((TRC, LEV, ROWS, LO...  48.9 us
    unnamed x1, local copies, waits for them, and re-layouts  1.87 us

profile of v2, /device:TPU:1, one launch (start us, length us, event | category | flops | bytes accessed | tf_op | source)
XLA Modules:
  0.0 50.8 jit_solution(7602434762280105239)
XLA Ops:
  0.0 48.9 %shard_map.73 = f32[8,4,8,512]{3,2,1,0:T(8,128)} custom-call(f32[8,4,8,512]{3,2,1,0:T(8,128)} %tracers.1, f32[2,1,3,4,8,512]{5,4,3,2,1,0:T(8,128)} %transports.1, f32[2,1,4,8,512]{4,3,2,1,0:T(8,128)} %thickness.1, s32[2]{0:T(128)} %owner.1, s32[8,512]{1,0:T(8,128)} %land_sea.1, s32[8]{0:T(128)} %pairs.1, f32[8]{0:T(128)} %rates.1), custom_call_target="tpu_custom_call" | custom-call | tf_op jit(solution)/shard_map/pallas_call | solution.py:429
  48.9 1.9 %copy.9 = f32[8,4,8,512]{3,2,1,0:T(8,128)} copy(f32[8,4,8,512]{3,2,1,0:T(8,128)} %shard_map.73) | data formatting | bytes 1048576

commit v3 on v2

--- a/solution.py
+++ b/solution.py
@@ -14,8 +14,6 @@
 
 GROUPS = (((0, 1), (0, -1)), ((0, 0), (0, 2)), ((1, 1), (1, -1)), ((1, 0), (1, 2)))
 
-TILES = (3, 2, 3, 2)
-
 
 def limited(left, right):
     two_l, two_r = 2.0 * jnp.abs(left), 2.0 * jnp.abs(right)
@@ -39,8 +37,8 @@
 
 def kernel(
     tracers, transports, thickness, owner, land_sea, pairs, rates, out,
-    stage, halo_rec, recv0, recv_halo0, along_y1, along_y2, along_y3, along_z1, along_z2, along_z3,
-    quarter1, quarter2, quarter3, part1, part2, part3, sel, rec_a, rec_b, sea_int, sea_halo_int,
+    stage, recv0, along_y1, along_y2, along_y3, along_z1, along_z2, along_z3,
+    quarter1, quarter2, quarter3, part2, part3, part1, sel, border0, border1, rec_a, rec_b, sea_int, sea_halo_int,
     field_a, field_b, mid, mid2, done,
     c_mer, c_zon, c_ver, w_mer, w_zon, w_ver, depth,
     owner_s, pairs_s, rates_s,
@@ -124,12 +122,31 @@
     def all_bytes(sems, like):
         pltpu.make_async_copy(like, like, sems).wait()
 
+    for_north, for_south = pl.ds(0, 1), pl.ds(1, 2)
+
+    def put_border(border, tile):
+        border[0:1], border[1:2], border[2:3] = tile[1, 7:8], tile[1, 0:1], tile[0, 0:1]
+
     three = pl.ds(0, 3)
-    likes = {0: recv0.at[pl.ds(0, 15)], 1: recv_halo0.at[pl.ds(0, 15)], 2: stage.at[three, pl.ds(0, 15), 0]}
-    for g in (1, 2, 3):
-        first = 8 + 4 * g
-        likes[first] = likes[first + 3] = along_y[g].at[three]
-        likes[first + 1] = likes[first + 2] = along_z[g].at[three]
+    likes = {
+        0: recv0.at[pl.ds(0, 15)],
+        1: recv0.at[pl.ds(0, 15)],
+        2: rec_a.at[0, :, 2, for_north],
+        3: rec_a.at[0, :, 2, for_south],
+        4: part2.at[:, 2, for_north],
+        5: part2.at[:, 2, for_south],
+        12: along_y1.at[three],
+        13: along_z1.at[three],
+        15: along_y1.at[three],
+        16: along_y2.at[three],
+        17: along_z2.at[three],
+        18: along_z2.at[three],
+        19: rec_a.at[1, three],
+        20: along_y3.at[three],
+        21: along_z3.at[three],
+        22: along_z3.at[three],
+        23: along_y3.at[three],
+    }
 
     def arrived(sem):
         all_bytes(recv_sem.at[sem], likes[sem])
@@ -140,56 +157,59 @@
 
     def scatter_y(g):
         staged(g)
-        own = pl.ds(4 * my_y, 4)
-        if TILES[g] == 3:
-            along("y", lambda y: stage.at[g, pl.ds(4 * y, 4)], along_y[g].at[my_y, :, pl.ds(0, 2)], 8 + 4 * g)
-            along("y", lambda y: halo_rec.at[1, :, :, lanes(y)], along_y[g].at[my_y, :, 2], 8 + 4 * g)
-            along_y[g][my_y, :, 0:2] = stage[g, own]
-            along_y[g][my_y, :, 2] = halo_rec[1, :, :, lanes(my_y)]
-        else:
-            along("y", lambda y: stage.at[g, pl.ds(4 * y, 4)], along_y[g].at[my_y], 8 + 4 * g)
-            along_y[g][my_y] = stage[g, own]
+        along("y", lambda y: stage.at[g, pl.ds(4 * y, 4)], along_y[g].at[my_y], 8 + 4 * g)
+        along_y[g][my_y] = stage[g, pl.ds(4 * my_y, 4)]
 
     def scatter_z(g):
         arrived(8 + 4 * g)
         quarter[g][...] = along_y[g][owner_s[g // 2] // 4]
-        along("z", lambda z: quarter[g].at[z], along_z[g].at[my_z], 9 + 4 * g)
-        along_z[g][my_z] = quarter[g][my_z]
+        if g == 1:
+            along("z", lambda z: quarter1, along_z1.at[my_z], 13)
+            along_z1[my_z] = quarter1[...]
+        else:
+            along("z", lambda z: quarter[g].at[z], along_z[g].at[my_z], 9 + 4 * g)
+            along_z[g][my_z] = quarter[g][my_z]
 
     def gather_z(g):
         arrived(9 + 4 * g)
-        part[g][my_z] = along_z[g][lax.rem(owner_s[g // 2], 4)]
-        along("z", lambda z: part[g].at[my_z], part[g].at[my_z], 10 + 4 * g)
+        chosen = along_z[g][lax.rem(owner_s[g // 2], 4)]
+        if g == 1:
+            part1[...] = chosen
+            return
+        both = pl.ds(0, 2)
+        part[g][my_z, 0:2] = chosen
+        along("z", lambda z: part[g].at[my_z, both], part[g].at[my_z, both], 10 + 4 * g)
+        if g == 2:
+            put_border(border1, chosen)
+            for k in range(4):
+                there = my_y * 4 + lax.rem(my_z + k, 4)
+                one_copy(border1.at[for_north], part2.at[my_z, 2, for_north], 4, lat=north, trc=there).start()
+                one_copy(border1.at[for_south], part2.at[my_z, 2, for_south], 5, lat=south, trc=there).start()
 
     def gather_y(g):
-        arrived(10 + 4 * g)
-        rec = (rec_a if TILES[g] == 3 else rec_b).at[g // 2]
+        if g > 1:
+            arrived(10 + 4 * g)
+        if g == 2:
+            arrived(4)
+            arrived(5)
+        rec = (rec_a if g == 2 else rec_b).at[g // 2]
         along("y", lambda y: part[g], rec.at[:, :, :, lanes(my_y)], 11 + 4 * g)
         rec[:, :, :, lanes(my_y)] = part[g][...]
 
     staged(0)
     to_peers(lambda peer: stage.at[0, peer], recv0.at[me], 0)
     recv0[me] = stage[0, me]
-    one, top = pl.ds(0, 1), pl.ds(7, 1)
+    scatter_y(1)
+    scatter_y(2)
+    scatter_y(3)
     rows = [
-        one_copy(thickness.at[:, 0, :, top], halo_rec.at[:, :, pl.ds(0, 1)], 3, lat=north),
-        one_copy(thickness.at[:, 0, :, one], halo_rec.at[:, :, pl.ds(1, 1)], 4, lat=south),
-        one_copy(transports.at[:, 0, 1, :, one], halo_rec.at[:, :, pl.ds(2, 1)], 5, lat=south),
-        one_copy(land_sea.at[top], sea_halo_int.at[pl.ds(0, 1)], 6, lat=north),
-        one_copy(land_sea.at[one], sea_halo_int.at[pl.ds(1, 1)], 7, lat=south),
+        one_copy(land_sea.at[pl.ds(7, 1)], sea_halo_int.at[pl.ds(0, 1)], 6, lat=north),
+        one_copy(land_sea.at[pl.ds(0, 1)], sea_halo_int.at[pl.ds(1, 1)], 7, lat=south),
     ]
     for copy in rows:
         copy.start()
-    scatter_y(1)
     for copy in smalls:
         copy.wait()
-    for copy in rows[:3]:
-        copy.wait()
-    to_peers(lambda peer: halo_rec.at[0, peer % 4, :, lanes(peer // 4)], recv_halo0.at[me], 1)
-    recv_halo0[me] = halo_rec[0, my_z, :, lanes(my_y)]
-    scatter_y(2)
-    scatter_y(3)
-    scatter_z(1)
 
     def field_halos(field, sem):
         return [
@@ -212,20 +232,31 @@
     for copy in halos:
         copy.start()
 
-    arrived(0)
-    arrived(1)
-    sel[0:2] = recv0[owner_s[0]]
-    sel[2] = recv_halo0[owner_s[0]]
-    to_peers(lambda peer: sel, rec_a.at[0, my_z, :, :, lanes(my_y)], 2)
-    rec_a[0, my_z, :, :, lanes(my_y)] = sel[...]
+    scatter_z(1)
     scatter_z(2)
     scatter_z(3)
-    gather_z(1)
+    arrived(0)
+    chosen = recv0[owner_s[0]]
+    sel[...] = chosen
+    put_border(border0, chosen)
+    both = pl.ds(0, 2)
+    to_peers(lambda peer: sel, rec_a.at[0, my_z, both, :, lanes(my_y)], 1)
+
+    def borders(k, _):
+        there = lax.rem(me + k, RING)
+        for part_of, sem, where in ((for_north, 2, north), (for_south, 3, south)):
+            target = rec_a.at[0, my_z, 2, part_of, lanes(my_y)]
+            one_copy(border0.at[part_of], target, sem, lat=where, trc=there).start()
+        return 0
+
+    lax.fori_loop(0, RING, borders, 0)
+    rec_a[0, my_z, 0:2, :, lanes(my_y)] = chosen
     gather_z(2)
     gather_z(3)
+    gather_z(1)
     gather_y(1)
 
-    for copy in rows[3:]:
+    for copy in rows:
         copy.wait_recv()
     sub = lax.broadcasted_iota(jnp.int32, (ROWS, LON), 0)
     sea = sea_int[...].astype(F32)
@@ -381,7 +412,8 @@
             zonal_row(r)
             vertical_row(r, target, offset)
 
-    arrived(2)
+    for sem in (1, 2, 3):
+        arrived(sem)
     mer_terms(0)
     for copy in halos:
         copy.wait()
@@ -408,16 +440,17 @@
     arrived(23)
     zon_terms(1)
     ver_terms(1)
-    run_rows(0, ROWS, done, 0)
-    stores = [
-        pltpu.make_async_copy(done.at[:, :, t], out.at[t], local_sem.at[36 + t])
-        for t in range(TRC)
-    ]
-    for copy in stores:
-        copy.start()
+    stores = []
+    for half in range(2):
+        run_rows(4 * half, 4 * half + 4, done, 0)
+        part_of = pl.ds(4 * half, 4)
+        for t in range(TRC):
+            sem = local_sem.at[36 + 8 * half + t]
+            stores.append(pltpu.make_async_copy(done.at[:, part_of, t], out.at[t, :, part_of], sem))
+            stores[-1].start()
     for sem, like in likes.items():
         all_bytes(send_sem.at[sem], like)
-    for copy in rows[3:]:
+    for copy in rows:
         copy.wait_send()
     for copy in stores:
         copy.wait()
@@ -433,14 +466,15 @@
         out_specs=any_space,
         scratch_shapes=[
             vmem((4, RING, 2, ROWS, BLK), F32),
-            vmem((STEPS, LEV, ROWS, LON), F32),
             vmem((RING, 2, ROWS, BLK), F32),
-            vmem((RING, ROWS, BLK), F32),
-            *[vmem((4, 4, n, ROWS, BLK), F32) for n in TILES[1:]],
-            *[vmem((4, n, ROWS, BLK), F32) for n in TILES[1:]],
-            *[vmem((4, n, ROWS, BLK), F32) for n in TILES[1:]],
-            *[vmem((4, n, ROWS, BLK), F32) for n in TILES[1:]],
-            vmem((3, ROWS, BLK), F32),
+            *[vmem((4, 4, 2, ROWS, BLK), F32)] * 3,
+            vmem((4, 4, 2, ROWS, BLK), F32),
+            *[vmem((4, 2, ROWS, BLK), F32)] * 2,
+            *[vmem((4, 2, ROWS, BLK), F32)] * 3,
+            vmem((4, 3, ROWS, BLK), F32),
+            *[vmem((4, 2, ROWS, BLK), F32)] * 2,
+            vmem((2, ROWS, BLK), F32),
+            *[vmem((ROWS, BLK), F32)] * STEPS,
             vmem((STEPS, LEV, 3, ROWS, LON), F32),
             vmem((STEPS, LEV, 2, ROWS, LON), F32),
             vmem((ROWS, LON), jnp.int32),
@@ -460,7 +494,7 @@
             pltpu.SMEM((STEPS,), jnp.int32),
             pltpu.SMEM((TRC,), jnp.int32),
             pltpu.SMEM((TRC,), F32),
-            pltpu.SemaphoreType.DMA((44,)),
+            pltpu.SemaphoreType.DMA((52,)),
             pltpu.SemaphoreType.DMA((24,)),
             pltpu.SemaphoreType.DMA((24,)),
         ],

time: 50.9 us -> 47.9 us (0.941); the launches traced: 50.8 us -> 47.1 us
  Pallas kernels: 48.9 us -> 45.2 us
    pallas_call x1, Pallas kernels: 48.9 us -> 45.2 us  [per_device(): pl.pallas_call(kernel, out_shape=jax.ShapeDtypeStruct((TRC, LEV, ROWS, LO...]
where the time goes in v3:
time: 47.9 us; the launch traced here: 47.1 us
  Pallas kernels  45.2 us (94%)
  local copies, waits for them, and re-layouts  1.87 us (4%)
    pallas_call x1, Pallas kernels, per_device(): pl.pallas_call(kernel, out_shape=jax.ShapeDtypeStruct((TRC, LEV, ROWS, LO...  45.2 us
    unnamed x1, local copies, waits for them, and re-layouts  1.87 us

profile of v3, /device:TPU:1, one launch (start us, length us, event | category | flops | bytes accessed | tf_op | source)
XLA Modules:
  0.0 47.1 jit_solution(12790875175112446432)
XLA Ops:
  0.0 45.2 %shard_map.73 = f32[8,4,8,512]{3,2,1,0:T(8,128)} custom-call(f32[8,4,8,512]{3,2,1,0:T(8,128)} %tracers.1, f32[2,1,3,4,8,512]{5,4,3,2,1,0:T(8,128)} %transports.1, f32[2,1,4,8,512]{4,3,2,1,0:T(8,128)} %thickness.1, s32[2]{0:T(128)} %owner.1, s32[8,512]{1,0:T(8,128)} %land_sea.1, s32[8]{0:T(128)} %pairs.1, f32[8]{0:T(128)} %rates.1), custom_call_target="tpu_custom_call" | custom-call | tf_op jit(solution)/shard_map/pallas_call | solution.py:462
  45.2 1.9 %copy.9 = f32[8,4,8,512]{3,2,1,0:T(8,128)} copy(f32[8,4,8,512]{3,2,1,0:T(8,128)} %shard_map.73) | data formatting | bytes 1048576

commit v4 on v2

--- a/solution.py
+++ b/solution.py
@@ -14,8 +14,6 @@
 
 GROUPS = (((0, 1), (0, -1)), ((0, 0), (0, 2)), ((1, 1), (1, -1)), ((1, 0), (1, 2)))
 
-TILES = (3, 2, 3, 2)
-
 
 def limited(left, right):
     two_l, two_r = 2.0 * jnp.abs(left), 2.0 * jnp.abs(right)
@@ -39,15 +37,16 @@
 
 def kernel(
     tracers, transports, thickness, owner, land_sea, pairs, rates, out,
-    stage, halo_rec, recv0, recv_halo0, along_y1, along_y2, along_y3, along_z1, along_z2, along_z3,
-    quarter1, quarter2, quarter3, part1, part2, part3, sel, rec_a, rec_b, sea_int, sea_halo_int,
-    field_a, field_b, mid, mid2, done,
+    stage, along_y0, along_y1, along_y2, along_y3, along_z0, along_z1, along_z2, along_z3,
+    quarter0, quarter1, quarter2, quarter3, part0, part1, part2, part3, border0, border1, rec_a, rec_b, sea_int, sea_halo_int,
+    field_a, field_b, dev_l, dev_r, mid, mid2, done,
     c_mer, c_zon, c_ver, w_mer, w_zon, w_ver, depth,
     owner_s, pairs_s, rates_s,
     local_sem, send_sem, recv_sem,
 ):
-    along_y, along_z = (None, along_y1, along_y2, along_y3), (None, along_z1, along_z2, along_z3)
-    quarter, part = (None, quarter1, quarter2, quarter3), (None, part1, part2, part3)
+    along_y, along_z = (along_y0, along_y1, along_y2, along_y3), (along_z0, along_z1, along_z2, along_z3)
+    quarter, part = (quarter0, quarter1, quarter2, quarter3), (part0, part1, part2, part3)
+    border = (border0, None, border1)
     lat, me = lax.axis_index("lat"), lax.axis_index("trc")
     my_y, my_z = me // 4, me % 4
     north, south = lax.rem(lat + 1, RING), lax.rem(lat + RING - 1, RING)
@@ -57,14 +56,11 @@
 
     barrier = pltpu.get_barrier_semaphore()
 
-    def greet(k, _):
-        peer = lax.rem(me + k, RING)
-        pl.semaphore_signal(barrier, inc=1, device_id={"trc": peer}, device_id_type=MESH)
-        return 0
-
     for beside in (north, south):
         pl.semaphore_signal(barrier, inc=1, device_id={"lat": beside}, device_id_type=MESH)
-    lax.fori_loop(1, RING, greet, 0)
+    for k in range(1, 4):
+        for peer in (my_y * 4 + lax.rem(my_z + k, 4), lax.rem(my_y + k, 4) * 4 + my_z):
+            pl.semaphore_signal(barrier, inc=1, device_id={"trc": peer}, device_id_type=MESH)
 
     stages = []
     for g, fields in enumerate(GROUPS):
@@ -97,20 +93,12 @@
     for copy in smalls + loads:
         copy.start()
 
-    pl.semaphore_wait(barrier, RING + 1)
+    pl.semaphore_wait(barrier, 8)
 
     def one_copy(source, target, sem, **where):
         return pltpu.make_async_remote_copy(
             source, target, send_sem.at[sem], recv_sem.at[sem], device_id=where, device_id_type=MESH
         )
-
-    def to_peers(source, target, sem):
-        def one(k, _):
-            peer = lax.rem(me + k, RING)
-            one_copy(source(peer), target, sem, trc=peer).start()
-            return 0
-
-        lax.fori_loop(1, RING, one, 0)
 
     def along(axis, source, target, sem):
         for k in (2, 1, 3):
@@ -124,72 +112,60 @@
     def all_bytes(sems, like):
         pltpu.make_async_copy(like, like, sems).wait()
 
+    for_north, for_south = pl.ds(0, 1), pl.ds(1, 2)
+
+    def put_border(rows, tile):
+        rows[0:1], rows[1:2], rows[2:3] = tile[1, 7:8], tile[1, 0:1], tile[0, 0:1]
+
     three = pl.ds(0, 3)
-    likes = {0: recv0.at[pl.ds(0, 15)], 1: recv_halo0.at[pl.ds(0, 15)], 2: stage.at[three, pl.ds(0, 15), 0]}
-    for g in (1, 2, 3):
-        first = 8 + 4 * g
-        likes[first] = likes[first + 3] = along_y[g].at[three]
-        likes[first + 1] = likes[first + 2] = along_z[g].at[three]
+    likes = {s + 2 * i: rec_a.at[s, :, 2, rows] for s in range(STEPS) for i, rows in enumerate((for_north, for_south))}
+    for g in range(4):
+        for k in range(3):
+            likes[12 + 3 * g + k] = along_y[g].at[three]
 
     def arrived(sem):
         all_bytes(recv_sem.at[sem], likes[sem])
 
-    def staged(g):
+    def scatter_y(g):
         for copy in stages[g]:
             copy.wait()
-
-    def scatter_y(g):
-        staged(g)
-        own = pl.ds(4 * my_y, 4)
-        if TILES[g] == 3:
-            along("y", lambda y: stage.at[g, pl.ds(4 * y, 4)], along_y[g].at[my_y, :, pl.ds(0, 2)], 8 + 4 * g)
-            along("y", lambda y: halo_rec.at[1, :, :, lanes(y)], along_y[g].at[my_y, :, 2], 8 + 4 * g)
-            along_y[g][my_y, :, 0:2] = stage[g, own]
-            along_y[g][my_y, :, 2] = halo_rec[1, :, :, lanes(my_y)]
-        else:
-            along("y", lambda y: stage.at[g, pl.ds(4 * y, 4)], along_y[g].at[my_y], 8 + 4 * g)
-            along_y[g][my_y] = stage[g, own]
-
-    def scatter_z(g):
-        arrived(8 + 4 * g)
+        along("y", lambda y: stage.at[g, pl.ds(4 * y, 4)], along_y[g].at[my_y], 12 + 3 * g)
+        along_y[g][my_y] = stage[g, pl.ds(4 * my_y, 4)]
+
+    def spread_z(g):
+        arrived(12 + 3 * g)
         quarter[g][...] = along_y[g][owner_s[g // 2] // 4]
-        along("z", lambda z: quarter[g].at[z], along_z[g].at[my_z], 9 + 4 * g)
-        along_z[g][my_z] = quarter[g][my_z]
-
-    def gather_z(g):
-        arrived(9 + 4 * g)
-        part[g][my_z] = along_z[g][lax.rem(owner_s[g // 2], 4)]
-        along("z", lambda z: part[g].at[my_z], part[g].at[my_z], 10 + 4 * g)
+        along("z", lambda z: quarter[g], along_z[g].at[my_z], 13 + 3 * g)
+        along_z[g][my_z] = quarter[g][...]
 
     def gather_y(g):
-        arrived(10 + 4 * g)
-        rec = (rec_a if TILES[g] == 3 else rec_b).at[g // 2]
-        along("y", lambda y: part[g], rec.at[:, :, :, lanes(my_y)], 11 + 4 * g)
-        rec[:, :, :, lanes(my_y)] = part[g][...]
-
-    staged(0)
-    to_peers(lambda peer: stage.at[0, peer], recv0.at[me], 0)
-    recv0[me] = stage[0, me]
-    one, top = pl.ds(0, 1), pl.ds(7, 1)
+        arrived(13 + 3 * g)
+        part[g][...] = along_z[g][lax.rem(owner_s[g // 2], 4)]
+        s, first = g // 2, g % 2 == 0
+        rec = (rec_a if first else rec_b).at[s, :, pl.ds(0, 2), :, lanes(my_y)]
+        along("y", lambda y: part[g], rec, 14 + 3 * g)
+        if first:
+            for l in range(LEV):
+                put_border(border[g].at[l], part[g][l])
+            for k in (2, 1, 3, 0):
+                there = lax.rem(my_y + k, 4) * 4 + my_z
+                for part_of, sem, where in ((for_north, s, north), (for_south, s + 2, south)):
+                    target = rec_a.at[s, :, 2, part_of, lanes(my_y)]
+                    one_copy(border[g].at[:, part_of], target, sem, lat=where, trc=there).start()
+        rec[...] = part[g][...]
+
+    for g in range(4):
+        scatter_y(g)
     rows = [
-        one_copy(thickness.at[:, 0, :, top], halo_rec.at[:, :, pl.ds(0, 1)], 3, lat=north),
-        one_copy(thickness.at[:, 0, :, one], halo_rec.at[:, :, pl.ds(1, 1)], 4, lat=south),
-        one_copy(transports.at[:, 0, 1, :, one], halo_rec.at[:, :, pl.ds(2, 1)], 5, lat=south),
-        one_copy(land_sea.at[top], sea_halo_int.at[pl.ds(0, 1)], 6, lat=north),
-        one_copy(land_sea.at[one], sea_halo_int.at[pl.ds(1, 1)], 7, lat=south),
+        one_copy(land_sea.at[pl.ds(7, 1)], sea_halo_int.at[pl.ds(0, 1)], 6, lat=north),
+        one_copy(land_sea.at[pl.ds(0, 1)], sea_halo_int.at[pl.ds(1, 1)], 7, lat=south),
     ]
     for copy in rows:
         copy.start()
-    scatter_y(1)
     for copy in smalls:
         copy.wait()
-    for copy in rows[:3]:
-        copy.wait()
-    to_peers(lambda peer: halo_rec.at[0, peer % 4, :, lanes(peer // 4)], recv_halo0.at[me], 1)
-    recv_halo0[me] = halo_rec[0, my_z, :, lanes(my_y)]
-    scatter_y(2)
-    scatter_y(3)
-    scatter_z(1)
+    spread_z(0)
+    spread_z(1)
 
     def field_halos(field, sem):
         return [
@@ -197,11 +173,12 @@
             one_copy(field.at[:, pl.ds(3, 3)], field.at[:, pl.ds(11, 3)], sem + 1, lat=south),
         ]
 
-    def clear_ends(field):
+    def clear_south(field):
         @pl.when(lat == 0)
         def _():
             field[:, 0:3] = jnp.zeros((LEV, 3, TRC, LON), F32)
 
+    def clear_north(field):
         @pl.when(lat == RING - 1)
         def _():
             field[:, 11:14] = jnp.zeros((LEV, 3, TRC, LON), F32)
@@ -212,20 +189,10 @@
     for copy in halos:
         copy.start()
 
-    arrived(0)
-    arrived(1)
-    sel[0:2] = recv0[owner_s[0]]
-    sel[2] = recv_halo0[owner_s[0]]
-    to_peers(lambda peer: sel, rec_a.at[0, my_z, :, :, lanes(my_y)], 2)
-    rec_a[0, my_z, :, :, lanes(my_y)] = sel[...]
-    scatter_z(2)
-    scatter_z(3)
-    gather_z(1)
-    gather_z(2)
-    gather_z(3)
-    gather_y(1)
-
-    for copy in rows[3:]:
+    spread_z(2)
+    spread_z(3)
+
+    for copy in rows:
         copy.wait_recv()
     sub = lax.broadcasted_iota(jnp.int32, (ROWS, LON), 0)
     sea = sea_int[...].astype(F32)
@@ -301,25 +268,37 @@
             + far * jnp.where(up, l0, r1)
         )
 
-    def meridional(field):
+    def columns(body):
         def column(i, _):
-            l, y = i // 4, lanes(i % 4)
-            q = [field[l, j, :, y] for j in range(14)]
-            d = [None] + [q[j] - q[j - 1] for j in range(1, 14)]
-            e = {f: edge_dev(d[f - 1], d[f], d[f + 1]) for f in range(2, 13)}
-            dev = {j: limited(e[j] - d[j], e[j + 1]) for j in range(2, 12)}
-            across = []
-            for f in range(3, 12):
-                r = pl.ds(f - 3, 1)
-                terms = [wide(c_mer, k, l, r, y) for k in range(3)]
+            body(i // 4, lanes(i % 4))
+            return 0
+
+        lax.fori_loop(0, LEV * 4, column, 0)
+
+    def reconstruct(field, first, last):
+        def body(l, y):
+            q = {j: field[l, j, :, y] for j in range(first - 2, last + 2)}
+            d = {f: q[f] - q[f - 1] for f in range(first - 1, last + 2)}
+            e = {f: edge_dev(d[f - 1], d[f], d[f + 1]) for f in range(first, last + 1)}
+            for j in range(first, last):
+                dev_l[l, j, :, y], dev_r[l, j, :, y] = limited(e[j] - d[j], e[j + 1])
+
+        columns(body)
+
+    def meridional(field, first, last):
+        def body(l, y):
+            q = {j: field[l, j, :, y] for j in range(first + 2, last + 4)}
+            dev = {j: (dev_l[l, j, :, y], dev_r[l, j, :, y]) for j in range(first + 2, last + 4)}
+            across = {}
+            for f in range(first + 3, last + 4):
+                terms = [wide(c_mer, k, l, pl.ds(f - 3, 1), y) for k in range(3)]
                 (l0, r0), (l1, r1) = dev[f - 1], dev[f]
-                across.append(flux(*terms, q[f - 1], r0, l0, q[f], l1, r1))
-            for r in range(ROWS):
+                across[f] = flux(*terms, q[f - 1], r0, l0, q[f], l1, r1)
+            for r in range(first, last):
                 kept, inv = (wide(w_mer, k, l, pl.ds(r, 1), y) for k in range(2))
-                mid[l, r, :, y] = kept * q[r + 3] + inv * (across[r] - across[r + 1])
-            return 0
-
-        lax.fori_loop(0, LEV * 4, column, 0)
+                mid[l, r, :, y] = kept * q[r + 3] + inv * (across[r + 3] - across[r + 4])
+
+        columns(body)
 
     lane = lax.broadcasted_iota(jnp.int32, (TRC, BLK), 1)
 
@@ -381,43 +360,61 @@
             zonal_row(r)
             vertical_row(r, target, offset)
 
-    arrived(2)
+    gather_y(0)
+    for copy in halos:
+        copy.wait_recv()
+    clear_south(field_a)
+    clear_north(field_a)
+    reconstruct(field_a, 2, 12)
+    gather_y(1)
+    for sem in (14, 0, 2):
+        arrived(sem)
     mer_terms(0)
-    for copy in halos:
-        copy.wait()
-    clear_ends(field_a)
-    meridional(field_a)
+    meridional(field_a, 0, ROWS)
     gather_y(2)
-    gather_y(3)
-    arrived(15)
+    arrived(17)
     zon_terms(0)
     ver_terms(0)
-    halos = field_halos(field_b, 10)
+    next_halos = field_halos(field_b, 10)
     run_rows(0, 3, field_b, 3)
-    halos[1].start()
+    next_halos[1].start()
+    gather_y(3)
     run_rows(5, 8, field_b, 3)
-    halos[0].start()
+    next_halos[0].start()
     run_rows(3, 5, field_b, 3)
 
-    arrived(19)
+    reconstruct(field_b, 5, 9)
+    for sem in (20, 1, 3):
+        arrived(sem)
     mer_terms(1)
-    for copy in halos:
-        copy.wait()
-    clear_ends(field_b)
-    meridional(field_b)
+    next_halos[1].wait_recv()
+    clear_north(field_b)
+    reconstruct(field_b, 9, 12)
+    meridional(field_b, 3, ROWS)
     arrived(23)
     zon_terms(1)
     ver_terms(1)
-    run_rows(0, ROWS, done, 0)
-    stores = [
-        pltpu.make_async_copy(done.at[:, :, t], out.at[t], local_sem.at[36 + t])
-        for t in range(TRC)
-    ]
-    for copy in stores:
-        copy.start()
+    stores = []
+
+    def finish(first, last):
+        run_rows(first, last, done, 0)
+        part_of = pl.ds(first, last - first)
+        for t in range(TRC):
+            sem = local_sem.at[36 + len(stores)]
+            stores.append(pltpu.make_async_copy(done.at[:, part_of, t], out.at[t, :, part_of], sem))
+            stores[-1].start()
+
+    finish(3, ROWS)
+    next_halos[0].wait_recv()
+    clear_south(field_b)
+    reconstruct(field_b, 2, 5)
+    meridional(field_b, 0, 3)
+    finish(0, 3)
+    for copy in halos + next_halos:
+        copy.wait_send()
     for sem, like in likes.items():
         all_bytes(send_sem.at[sem], like)
-    for copy in rows[3:]:
+    for copy in rows:
         copy.wait_send()
     for copy in stores:
         copy.wait()
@@ -433,18 +430,17 @@
         out_specs=any_space,
         scratch_shapes=[
             vmem((4, RING, 2, ROWS, BLK), F32),
-            vmem((STEPS, LEV, ROWS, LON), F32),
-            vmem((RING, 2, ROWS, BLK), F32),
-            vmem((RING, ROWS, BLK), F32),
-            *[vmem((4, 4, n, ROWS, BLK), F32) for n in TILES[1:]],
-            *[vmem((4, n, ROWS, BLK), F32) for n in TILES[1:]],
-            *[vmem((4, n, ROWS, BLK), F32) for n in TILES[1:]],
-            *[vmem((4, n, ROWS, BLK), F32) for n in TILES[1:]],
-            vmem((3, ROWS, BLK), F32),
+            *[vmem((4, 4, 2, ROWS, BLK), F32)] * 4,
+            *[vmem((4, 4, 2, ROWS, BLK), F32)] * 4,
+            *[vmem((4, 2, ROWS, BLK), F32)] * 4,
+            *[vmem((4, 2, ROWS, BLK), F32)] * 4,
+            *[vmem((LEV, ROWS, BLK), F32)] * STEPS,
             vmem((STEPS, LEV, 3, ROWS, LON), F32),
             vmem((STEPS, LEV, 2, ROWS, LON), F32),
             vmem((ROWS, LON), jnp.int32),
             vmem((ROWS, LON), jnp.int32),
+            vmem((LEV, 14, TRC, LON), F32),
+            vmem((LEV, 14, TRC, LON), F32),
             vmem((LEV, 14, TRC, LON), F32),
             vmem((LEV, 14, TRC, LON), F32),
             vmem((LEV, ROWS, TRC, LON), F32),
@@ -460,7 +456,7 @@
             pltpu.SMEM((STEPS,), jnp.int32),
             pltpu.SMEM((TRC,), jnp.int32),
             pltpu.SMEM((TRC,), F32),
-            pltpu.SemaphoreType.DMA((44,)),
+            pltpu.SemaphoreType.DMA((52,)),
             pltpu.SemaphoreType.DMA((24,)),
             pltpu.SemaphoreType.DMA((24,)),
         ],

time: 50.9 us -> 46 us (0.904)
  the two profiles are of different devices: /device:TPU:1 before, /device:TPU:39 now
where the time goes in v4:
time: 46 us; the launch traced here: 45.9 us
  Pallas kernels  44 us (96%)
  local copies, waits for them, and re-layouts  1.87 us (4%)
    pallas_call x1, Pallas kernels, per_device(): pl.pallas_call(kernel, out_shape=jax.ShapeDtypeStruct((TRC, LEV, ROWS, LO...  44 us
    unnamed x1, local copies, waits for them, and re-layouts  1.87 us

profile of v4, /device:TPU:39, one launch (start us, length us, event | category | flops | bytes accessed | tf_op | source)
XLA Modules:
  0.0 45.9 jit_solution(9146676899428309575)
XLA Ops:
  0.0 44.0 %shard_map.73 = f32[8,4,8,512]{3,2,1,0:T(8,128)} custom-call(f32[8,4,8,512]{3,2,1,0:T(8,128)} %tracers.1, f32[2,1,3,4,8,512]{5,4,3,2,1,0:T(8,128)} %transports.1, f32[2,1,4,8,512]{4,3,2,1,0:T(8,128)} %thickness.1, s32[2]{0:T(128)} %owner.1, s32[8,512]{1,0:T(8,128)} %land_sea.1, s32[8]{0:T(128)} %pairs.1, f32[8]{0:T(128)} %rates.1), custom_call_target="tpu_custom_call" | custom-call | tf_op jit(solution)/shard_map/pallas_call | solution.py:426
  44.0 1.9 %copy.9 = f32[8,4,8,512]{3,2,1,0:T(8,128)} copy(f32[8,4,8,512]{3,2,1,0:T(8,128)} %shard_map.73) | data formatting | bytes 1048576

commit v5 on v4

--- a/solution.py
+++ b/solution.py
@@ -154,6 +154,28 @@
                     one_copy(border[g].at[:, part_of], target, sem, lat=where, trc=there).start()
         rec[...] = part[g][...]
 
+    def field_halos(field, sem):
+        return [
+            one_copy(field.at[:, pl.ds(8, 3)], field.at[:, pl.ds(0, 3)], sem, lat=north),
+            one_copy(field.at[:, pl.ds(3, 3)], field.at[:, pl.ds(11, 3)], sem + 1, lat=south),
+        ]
+
+    def clear_south(field):
+        @pl.when(lat == 0)
+        def _():
+            field[:, 0:3] = jnp.zeros((LEV, 3, TRC, LON), F32)
+
+    def clear_north(field):
+        @pl.when(lat == RING - 1)
+        def _():
+            field[:, 11:14] = jnp.zeros((LEV, 3, TRC, LON), F32)
+
+    for copy in loads:
+        copy.wait()
+    halos = field_halos(field_a, 8)
+    for copy in halos:
+        copy.start()
+
     for g in range(4):
         scatter_y(g)
     rows = [
@@ -167,30 +189,6 @@
     spread_z(0)
     spread_z(1)
 
-    def field_halos(field, sem):
-        return [
-            one_copy(field.at[:, pl.ds(8, 3)], field.at[:, pl.ds(0, 3)], sem, lat=north),
-            one_copy(field.at[:, pl.ds(3, 3)], field.at[:, pl.ds(11, 3)], sem + 1, lat=south),
-        ]
-
-    def clear_south(field):
-        @pl.when(lat == 0)
-        def _():
-            field[:, 0:3] = jnp.zeros((LEV, 3, TRC, LON), F32)
-
-    def clear_north(field):
-        @pl.when(lat == RING - 1)
-        def _():
-            field[:, 11:14] = jnp.zeros((LEV, 3, TRC, LON), F32)
-
-    for copy in loads:
-        copy.wait()
-    halos = field_halos(field_a, 8)
-    for copy in halos:
-        copy.start()
-
-    spread_z(2)
-    spread_z(3)
 
     for copy in rows:
         copy.wait_recv()
@@ -361,12 +359,14 @@
             vertical_row(r, target, offset)
 
     gather_y(0)
+    spread_z(2)
+    gather_y(1)
+    spread_z(3)
     for copy in halos:
         copy.wait_recv()
     clear_south(field_a)
     clear_north(field_a)
     reconstruct(field_a, 2, 12)
-    gather_y(1)
     for sem in (14, 0, 2):
         arrived(sem)
     mer_terms(0)

time: 46 us -> 42.6 us (0.926)
  the two profiles are of different devices: /device:TPU:39 before, /device:TPU:1 now
where the time goes in v5:
time: 42.6 us; the launch traced here: 42.4 us
  Pallas kernels  40.6 us (95%)
  local copies, waits for them, and re-layouts  1.87 us (4%)
    pallas_call x1, Pallas kernels, per_device(): pl.pallas_call(kernel, out_shape=jax.ShapeDtypeStruct((TRC, LEV, ROWS, LO...  40.6 us
    unnamed x1, local copies, waits for them, and re-layouts  1.87 us

profile of v5, /device:TPU:1, one launch (start us, length us, event | category | flops | bytes accessed | tf_op | source)
XLA Modules:
  0.0 42.4 jit_solution(727397049176494598)
XLA Ops:
  0.0 40.6 %shard_map.73 = f32[8,4,8,512]{3,2,1,0:T(8,128)} custom-call(f32[8,4,8,512]{3,2,1,0:T(8,128)} %tracers.1, f32[2,1,3,4,8,512]{5,4,3,2,1,0:T(8,128)} %transports.1, f32[2,1,4,8,512]{4,3,2,1,0:T(8,128)} %thickness.1, s32[2]{0:T(128)} %owner.1, s32[8,512]{1,0:T(8,128)} %land_sea.1, s32[8]{0:T(128)} %pairs.1, f32[8]{0:T(128)} %rates.1), custom_call_target="tpu_custom_call" | custom-call | tf_op jit(solution)/shard_map/pallas_call | solution.py:426
  40.6 1.9 %copy.9 = f32[8,4,8,512]{3,2,1,0:T(8,128)} copy(f32[8,4,8,512]{3,2,1,0:T(8,128)} %shard_map.73) | data formatting | bytes 1048576

commit v6 on v5

--- a/solution.py
+++ b/solution.py
@@ -176,7 +176,7 @@
     for copy in halos:
         copy.start()
 
-    for g in range(4):
+    for g in range(2):
         scatter_y(g)
     rows = [
         one_copy(land_sea.at[pl.ds(7, 1)], sea_halo_int.at[pl.ds(0, 1)], 6, lat=north),
@@ -187,7 +187,9 @@
     for copy in smalls:
         copy.wait()
     spread_z(0)
+    scatter_y(2)
     spread_z(1)
+    scatter_y(3)
 
 
     for copy in rows:
@@ -361,7 +363,6 @@
     gather_y(0)
     spread_z(2)
     gather_y(1)
-    spread_z(3)
     for copy in halos:
         copy.wait_recv()
     clear_south(field_a)
@@ -369,6 +370,7 @@
     reconstruct(field_a, 2, 12)
     for sem in (14, 0, 2):
         arrived(sem)
+    spread_z(3)
     mer_terms(0)
     meridional(field_a, 0, ROWS)
     gather_y(2)

time: 42.6 us -> 41.6 us (0.977)
  Pallas kernels: 40.6 us -> 39.4 us
    pallas_call x1, Pallas kernels: 40.6 us -> 39.4 us  [per_device(): pl.pallas_call(kernel, out_shape=jax.ShapeDtypeStruct((TRC, LEV, ROWS, LO...]
where the time goes in v6:
time: 41.6 us; the launch traced here: 41.3 us
  Pallas kernels  39.4 us (95%)
  local copies, waits for them, and re-layouts  1.87 us (4%)
    pallas_call x1, Pallas kernels, per_device(): pl.pallas_call(kernel, out_shape=jax.ShapeDtypeStruct((TRC, LEV, ROWS, LO...  39.4 us
    unnamed x1, local copies, waits for them, and re-layouts  1.87 us

profile of v6, /device:TPU:1, one launch (start us, length us, event | category | flops | bytes accessed | tf_op | source)
XLA Modules:
  0.0 41.3 jit_solution(9285665760524245431)
XLA Ops:
  0.0 39.4 %shard_map.73 = f32[8,4,8,512]{3,2,1,0:T(8,128)} custom-call(f32[8,4,8,512]{3,2,1,0:T(8,128)} %tracers.1, f32[2,1,3,4,8,512]{5,4,3,2,1,0:T(8,128)} %transports.1, f32[2,1,4,8,512]{4,3,2,1,0:T(8,128)} %thickness.1, s32[2]{0:T(128)} %owner.1, s32[8,512]{1,0:T(8,128)} %land_sea.1, s32[8]{0:T(128)} %pairs.1, f32[8]{0:T(128)} %rates.1), custom_call_target="tpu_custom_call" | custom-call | tf_op jit(solution)/shard_map/pallas_call | solution.py:428
  39.4 1.9 %copy.9 = f32[8,4,8,512]{3,2,1,0:T(8,128)} copy(f32[8,4,8,512]{3,2,1,0:T(8,128)} %shard_map.73) | data formatting | bytes 1048576
